TPU v7x, 512 devices: a whole 4x4x16 slice. The times are simulated.
512 devices in a mesh: lat: 64 (over x, y, z_hi), lev: 8 (over z_lo, core).
Axes of the slice: x: 4, y: 4, z: 16 (z_hi: 4, z_lo: 4; z = z_hi * 4 + z_lo), core: 2. Of those that a mesh axis runs over, the one named last changes fastest.
Arguments:
- tracers: float32 [8, 8, 768, 1152], P(None, 'lev', 'lat'), may hold values from -6 to 6
- thickness: float32 [8, 768, 1152], P('lev', 'lat'), may hold values from 0.85 to 1.15
- courant_x: float32 [8, 768, 1152], P('lev', 'lat'), may hold values from -0.08 to 0.08
- courant_y: float32 [8, 768, 1152], P('lev', 'lat'), may hold values from -0.08 to 0.08
- level_weights: float32 [8], replicated, may hold values from 0.5 to 2
Outputs:
- remapped: float32 [8, 8, 768, 1152], P(None, None, 'lat', 'lev')
- column_mass: float32 [768, 1152], P('lat', 'lev')
All inputs are finite; a program needn't handle non-finite values.
Results may differ from a plain program's by a relative error of at most 0.0003.
Values sent between devices are 32-bit elements; how exact they have to be, the bound alone decides.
No kernel may reach another device: no remote copies, remote signals or barrier semaphores. Data moves between devices by JAX's collectives and lax.ppermute only.
A program may use at most 128 MiB of HBM per device.

v0:
```python
import math

import jax
import jax.numpy as jnp
from jax import lax
from jax.sharding import PartitionSpec as P


def with_halo(cells, sides, width):
    for axis, dim in sides:
        count = lax.axis_size(axis)
        ends = count - 1
        head = lax.slice_in_dim(cells, 0, width, axis=dim)
        tail = lax.slice_in_dim(cells, cells.shape[dim] - width, cells.shape[dim], axis=dim)
        cells = jnp.concatenate(
            [
                lax.ppermute(tail, axis, [(i, (i + 1) % count) for i in range(ends)]),
                cells,
                lax.ppermute(head, axis, [((i + 1) % count, i) for i in range(ends)]),
            ],
            axis=dim,
        )
    return cells


def swept_average(left_cell, right_cell, left_lo, middle, right_hi, courant):
    left_slope = middle - left_lo
    left_curve = 6.0 * (left_cell - 0.5 * (left_lo + middle))
    forward = middle - 0.5 * courant * (left_slope - (1.0 - 2.0 * courant / 3.0) * left_curve)
    reverse_c = -courant
    right_slope = right_hi - middle
    right_curve = 6.0 * (right_cell - 0.5 * (middle + right_hi))
    backward = middle + 0.5 * reverse_c * (
        right_slope + (1.0 - 2.0 * reverse_c / 3.0) * right_curve
    )
    return jnp.where(courant > 0.0, forward, backward)


def face_values(extended, courant, axis_dim):
    face_count = extended.shape[axis_dim] - 5

    def take_rows(offset, length):
        return lax.slice_in_dim(extended, offset, offset + length, axis=axis_dim)

    edge_values = 7.0 / 12.0 * (
        take_rows(1, face_count + 2) + take_rows(2, face_count + 2)
    ) - 1.0 / 12.0 * (take_rows(0, face_count + 2) + take_rows(3, face_count + 2))

    def edge_run(offset):
        return lax.slice_in_dim(edge_values, offset, offset + face_count, axis=axis_dim)

    return swept_average(
        take_rows(2, face_count),
        take_rows(3, face_count),
        edge_run(0),
        edge_run(1),
        edge_run(2),
        courant,
    )


def wrap_lon(field):
    return jnp.concatenate([field[..., -3:], field, field[..., :3]], axis=-1)


def centre_weights(first_row, row_count, lat_total):
    row_ids = (first_row + jnp.arange(row_count)).astype(jnp.float32)
    return jnp.sin(math.pi * (row_ids + 0.5) / lat_total)


def spectral_basis(lon_count):
    half_way = lon_count // 2
    column_ids = jnp.arange(lon_count)
    positions = jnp.arange(lon_count)
    wavenumber = jnp.where(column_ids <= half_way, column_ids, column_ids - half_way)
    phases = positions[:, None] * wavenumber[None] % lon_count
    angles = 2.0 * math.pi / lon_count * phases.astype(jnp.float32)
    basis = jnp.where(column_ids[None] <= half_way, jnp.cos(angles), jnp.sin(angles))
    weight = jnp.where(
        (column_ids == 0) | (column_ids == half_way), 1.0 / lon_count, 2.0 / lon_count
    )
    sines = jnp.sin(math.pi * wavenumber.astype(jnp.float32) / lon_count)
    safe_sq = jnp.where(wavenumber == 0, 1.0, sines * sines)
    return (basis, weight, wavenumber, safe_sq)


def damping_rows(centre, weight, wavenumber, safe_sq):
    factor = jnp.where(
        wavenumber[None] == 0, 1.0, jnp.minimum(1.0, 4.0 * centre[:, None] ** 2 / safe_sq[None])
    )
    return factor * weight[None]


def smooth(field, basis, scaled):
    spectrum = jnp.einsum("tlrn,nc->tlrc", field, basis, precision=lax.Precision.HIGHEST)
    spectrum = spectrum * scaled[None, None]
    return jnp.einsum("tlrc,nc->tlrn", spectrum, basis, precision=lax.Precision.HIGHEST)


def intersection_table(col_thick, level_weights):
    column_mass = jnp.sum(col_thick, axis=0)
    shares = level_weights / jnp.sum(level_weights)
    upper_edge = jnp.cumsum(col_thick, axis=0)
    lower_edge = upper_edge - col_thick
    target = shares[:, None, None] * column_mass[None]
    target_upper = jnp.cumsum(target, axis=0)
    target_lower = target_upper - target
    intersection = jnp.maximum(
        0.0,
        jnp.minimum(upper_edge[:, None], target_upper[None])
        - jnp.maximum(lower_edge[:, None], target_lower[None]),
    )
    return (intersection, target, column_mass)


def local(tracers, thickness, courant_x, courant_y, level_weights):
    tracer_count, level_count, row_count, lon_count = tracers.shape
    band_index = lax.axis_index("lat")
    band_total = lax.axis_size("lat")
    lat_total = row_count * band_total
    first_row = band_index * row_count
    centre = centre_weights(first_row, row_count, lat_total)
    face_ids = (first_row + jnp.arange(row_count + 1)).astype(jnp.float32)
    face_cos = jnp.sin(math.pi * face_ids / lat_total)
    stacked = jnp.concatenate([tracers, thickness[None], courant_y[None]], axis=0)
    extended = with_halo(stacked, (("lat", 2),), 3)
    cy_faces = extended[tracer_count + 1][:, 3 : row_count + 4]
    cx_faces = jnp.concatenate([courant_x, courant_x[:, :, :1]], axis=2)

    def div_x(flux):
        return flux[..., 1:] - flux[..., :-1]

    def div_y(flux):
        return (flux[..., 1:, :] - flux[..., :-1, :]) / centre[:, None]

    mass_x = cx_faces * face_values(wrap_lon(thickness), cx_faces, 2)
    mass_y = cy_faces * face_values(extended[tracer_count], cy_faces, 1) * face_cos[:, None]
    new_thick = thickness - div_x(mass_x) - div_y(mass_y)
    zonal = div_x(mass_x * face_values(wrap_lon(tracers), cx_faces, 3))
    merid = div_y(mass_y * face_values(extended[:tracer_count], cy_faces, 2))
    basis, weight, wavenumber, safe_sq = spectral_basis(lon_count)
    own_scaled = damping_rows(centre, weight, wavenumber, safe_sq)
    own_polar = jnp.min(centre) < 0.5
    zonal = lax.cond(
        own_polar, lambda field: smooth(field, basis, own_scaled), lambda field: field, zonal
    )
    ratios = (thickness[None] * tracers - zonal - merid) / new_thick[None]
    packed = jnp.concatenate([ratios, new_thick[None]], axis=0)
    columns = lax.all_to_all(packed, "lev", split_axis=3, concat_axis=1, tiled=True)
    col_ratios = columns[:tracer_count]
    intersection, target, column_mass = intersection_table(columns[tracer_count], level_weights)
    moved_mass = jnp.einsum(
        "tirc,ikrc->tkrc", col_ratios, intersection, precision=lax.Precision.HIGHEST
    )
    remapped = moved_mass / target[None]
    return (remapped, column_mass)


def solution(mesh):
    placed = (
        P(None, "lev", "lat", None),
        P("lev", "lat", None),
        P("lev", "lat", None),
        P("lev", "lat", None),
        P(),
    )
    return jax.shard_map(
        local,
        mesh=mesh,
        in_specs=placed,
        out_specs=(P(None, None, "lat", "lev"), P("lat", "lev")),
        check_vma=False,
    )
```

profile of v0, /device:TPU:30, one launch (start us, length us, event | category | flops | bytes accessed | tf_op | source)
XLA Modules:
  0.0 234.9 jit_solution(12576359717576882390)
XLA Ops:
  1.9 9.1 %collective-permute-start = (f32[10,1,3,1152]{3,1,2,0:T(1,128)S(1)}, f32[10,1,3,1152]{3,1,2,0:T(1,128)S(1)}, u32[]{:S(2)}, u32[]{:S(2)}) collective-permute-start(f32[10,1,3,1152]{3,1,2,0:T(1,128)S(1)} %get-tuple-element.211), channel_id=1, source_target_pairs={{0,8},{8,16},{16,24},{24,32},{32,40},{40,48},{48,56},{56,64},{64,7... | collective-permute-start | bytes 414728 | tf_op jit(solution)/shard_map/ppermute | solution.py:17
  11.0 5.7 %collective-permute-start.1 = (f32[10,1,3,1152]{3,1,2,0:T(1,128)S(1)}, f32[10,1,3,1152]{3,1,2,0:T(1,128)S(1)}, u32[]{:S(2)}, u32[]{:S(2)}) collective-permute-start(f32[10,1,3,1152]{3,1,2,0:T(1,128)S(1)} %get-tuple-element.212), channel_id=1, source_target_pairs={{8,0},{16,8},{24,16},{32,24},{40,32},{48,40},{56,48},{64,56},{72,6... | collective-permute-start | bytes 414728 | tf_op jit(solution)/shard_map/ppermute | solution.py:19
  21.3 1.3 fusion.93
  22.7 1.5 fusion.84
  26.1 4.4 %fusion.37 = f32[1152,1152]{1,0:T(8,128)} fusion(s32[1152]{0:T(1024)S(1)} %add_select_fusion.1), kind=kLoop, calls=%fused_computation.39 | loop fusion | flops 10616832 | bytes 5313024 | tf_op jit(solution)/shard_map/convert_element_type | solution.py:77
  31.9 52.2 %conditional.1 = (f32[8,1,12,1152]{3,0,2,1:T(8,128)S(1)}) conditional(s32[]{:T(128)} %convert_element_type.46, f32[8,1,12,1152]{3,2,0,1:T(8,128)S(1)} %slice_subtract_fusion, (pred[1,1152]{1,0:T(4,128)(4,1)S(1)}, pred[1,1152]{1,0:T(4,128)(4,1)S(1)}, f32[1152,1152]{1,0:T(8,128)}, f32[1152,1152]{1,0:T(8,128)}, f32[8,1,12,1152]{3,2,0,1:T(8,128)S(1)}, ...), branch_computations={%region_1.2_spmd, %region_2.3_spmd} | conditional | flops 3063132160 | bytes 29357768 | solution.py:144
  32.8 26.8 %fusion.19 = f32[8,12,1152]{2,1,0:T(8,128)S(1)} fusion(f32[1152,1152]{1,0:T(8,128)} %get-tuple-element.181, pred[1152]{0:T(1024)(128)(4,1)S(1)} %reduce.1, f32[8,1,12,1152]{3,2,0,1:T(8,128)S(1)} %get-tuple-element.173, f32[12,1152]{1,0:T(8,128)S(1)} %fusion.27), kind=kOutput, calls=%fused_computation.17 | convolution fusion | flops 1531588608 | bytes 6249600 | tf_op jit(solution)/shard_map/cond/branch_1_fun/tlrn,nc->tlrc/dot_general | solution.py:95
  59.6 24.1 %fusion.22 = f32[8,1,12,1152]{3,2,0,1:T(8,128)S(1)} fusion(f32[8,12,1152]{2,1,0:T(8,128)S(1)} %fusion.19, f32[1152,1152]{1,0:T(8,128)S(1)} %bitcast.96, pred[1152]{0:T(1024)(128)(4,1)S(1)} %reduce.5), kind=kOutput, calls=%fused_computation.18 | convolution fusion | flops 1531478016 | bytes 6194304 | tf_op jit(solution)/shard_map/cond/branch_1_fun/tlrc,nc->tlrn/dot_general | solution.py:97
  84.2 1.3 maximum_maximum_fusion
  86.9 1.7 pad_maximum_fusion.3
  90.1 9.4 %copy.179 = f32[9,1,12,1152]{2,1,0,3:T(1,128)} copy(f32[9,1,12,1152]{3,0,2,1:T(8,128)S(1)} %pad_maximum_fusion.2) | data formatting | bytes 995328 | tf_op jit(solution)/shard_map/concatenate | solution.py:148
  100.0 19.4 %reduce.11 = f32[1152,9,12]{2,1,0:T(8,128)} reduce(f32[1152,9,1,12]{3,2,1,0:T(1,128)} %bitcast.90, f32[]{:T(128)} %broadcast.417), dimensions={2}, to_apply=%bitcast.70.reduce_sub_computation | reduce | bytes 995332
  119.4 6.6 %reshape.448 = f32[8,1,15552]{2,1,0:T(1,128)} reshape(f32[1152,9,12]{2,1,0:T(8,128)} %reduce.11) | data formatting | bytes 995328
  126.0 3.7 %all-to-all-start = ((f32[8,1,15552]{2,1,0:T(1,128)}), f32[8,1,15552]{2,1,0:T(1,128)S(1)}, u32[]{:S(2)}, u32[]{:S(2)}) async-start(f32[8,1,15552]{2,1,0:T(1,128)} %reshape.448), calls=%async_computation | async-start | bytes 999424 | tf_op jit(solution)/shard_map/all_to_all | solution.py:149
  131.1 13.3 %all-to-all-done = f32[8,1,15552]{2,1,0:T(1,128)S(1)} async-done(((f32[8,1,15552]{2,1,0:T(1,128)}), f32[8,1,15552]{2,1,0:T(1,128)S(1)}, u32[]{:S(2)}, u32[]{:S(2)}) %all-to-all-start) | async-done | bytes 497696 | tf_op jit(solution)/shard_map/all_to_all | solution.py:149
  144.5 1.9 reduce.12
  146.4 11.5 %reshape.449 = f32[1152,9,1,12]{3,2,1,0:T(1,128)} reshape(f32[8,15552]{1,0:T(8,128)S(1)} %reduce.12) | data formatting | bytes 995328
  157.9 20.4 %bitcast_reduce_fusion = f32[9,12,1152]{1,0,2:T(8,128)} fusion(f32[1152,9,1,12]{3,2,1,0:T(1,128)} %reshape.449), kind=kLoop, calls=%fused_computation.177 | loop fusion | bytes 995328 | tf_op jit(solution)/shard_map/all_to_all | solution.py:149
  178.3 19.6 %copy.181 = f32[9,1,12,8,144]{3,0,4,2,1:T(8,128)} copy(f32[9,1,12,8,144]{2,0,4,3,1:T(8,128)} %bitcast.89) | data formatting | bytes 995328 | tf_op jit(solution)/shard_map/all_to_all | solution.py:149
  197.9 6.7 %fusion.104 = (f32[1,8,1,12,144]{1,0,4,3,2:T(1,128)S(1)}, f32[12,144]{1,0:T(8,128)S(1)}) fusion(f32[9,8,1,12,144]{1,0,4,3,2:T(8,128)} %bitcast.91), kind=kLoop, calls=%fused_computation.173 | loop fusion | flops 12096 | bytes 117504 | tf_op jit(solution)/shard_map/slice | solution.py:151
  204.7 2.4 %reduce_window_sum.17 = f32[8,12,144]{0,2,1:T(8,128)S(1)} reduce-window(f32[8,12,144]{0,2,1:T(8,128)S(1)} %bitcast.93, f32[]{:T(128)} %constant.118.clone.1), window={size=8x1x1 pad=7_0x0_0x0_0}, to_apply=%region_3.4 | reduce-window | flops 96768 | bytes 110596 | tf_op jit(solution)/shard_map/jit(cumsum)/reduce_window_sum | solution.py:103
  207.5 2.4 %reduce_window_sum.18 = f32[8,12,144]{0,2,1:T(8,128)S(1)} reduce-window(f32[8,12,144]{0,2,1:T(8,128)S(1)} %broadcast_multiply_fusion, f32[]{:T(128)} %constant.118.clone.1), window={size=8x1x1 pad=7_0x0_0x0_0}, to_apply=%region_6.7 | reduce-window | flops 96768 | bytes 110596 | tf_op jit(solution)/shard_map/jit(cumsum)/reduce_window_sum | solution.py:106
  210.8 17.4 %bitcast_divide_fusion = f32[8,8,12,144]{0,1,3,2:T(8,128)} fusion(f32[8,12,144]{0,2,1:T(8,128)S(1)} %broadcast_multiply_fusion, f32[9,8,1,12,144]{1,0,4,3,2:T(8,128)} %bitcast.92, f32[8,12,144]{0,2,1:T(8,128)S(1)} %fusion.83, f32[8,12,144]{0,2,1:T(8,128)S(1)} %sub.225, f32[8,12,144]{0,2,1:T(8,128)S(1)} %reduce_window_sum.18, ...), kind=kOutput, calls=%fused_computation.34 | convolution fusion | flops 11169792 | bytes 7796736 | tf_op jit(solution)/shard_map/tirc,ikrc->tkrc/dot_general | solution.py:152
  228.2 6.5 %copy.182 = f32[8,8,12,144]{3,1,2,0:T(8,128)} copy(f32[8,8,12,144]{0,1,3,2:T(8,128)} %bitcast_divide_fusion) | data formatting | bytes 884736
  (75 shorter events, 14.9 us)
Async XLA Ops:
  1.9 82.3 %collective-permute-start = (f32[10,1,3,1152]{3,1,2,0:T(1,128)S(1)}, f32[10,1,3,1152]{3,1,2,0:T(1,128)S(1)}, u32[]{:S(2)}, u32[]{:S(2)}) collective-permute-start(f32[10,1,3,1152]{3,1,2,0:T(1,128)S(1)} %get-tuple-element.211), channel_id=1, source_target_pairs={{0,8},{8,16},{16,24},{24,32},{32,40},{40,48},{48,56},{56,64},{64,7... | collective-permute-start | bytes 414728 | tf_op jit(solution)/shard_map/ppermute | solution.py:17
  11.0 73.2 %collective-permute-start.1 = (f32[10,1,3,1152]{3,1,2,0:T(1,128)S(1)}, f32[10,1,3,1152]{3,1,2,0:T(1,128)S(1)}, u32[]{:S(2)}, u32[]{:S(2)}) collective-permute-start(f32[10,1,3,1152]{3,1,2,0:T(1,128)S(1)} %get-tuple-element.212), channel_id=1, source_target_pairs={{8,0},{16,8},{24,16},{32,24},{40,32},{48,40},{56,48},{64,56},{72,6... | collective-permute-start | bytes 414728 | tf_op jit(solution)/shard_map/ppermute | solution.py:19
  25.2 5.9 %copy-start.1 = (f32[1,12,1152]{2,0,1:T(1,128)S(1)}, f32[1,12,1152]{2,0,1:T(1,128)}, u32[]{:S(2)}) copy-start(f32[1,12,1152]{2,0,1:T(1,128)} %param.8) | copy-start | bytes 165892
  31.9 52.3 %copy-start = (f32[8,1,12,1152]{3,1,2,0:T(1,128)S(1)}, f32[8,1,12,1152]{3,1,2,0:T(1,128)}, u32[]{:S(2)}) copy-start(f32[8,1,12,1152]{3,1,2,0:T(1,128)} %param.7) | copy-start | bytes 1327108
  31.9 52.3 %copy-start.2 = (f32[1,12,1152]{2,0,1:T(1,128)S(1)}, f32[1,12,1152]{2,0,1:T(1,128)}, u32[]{:S(2)}) copy-start(f32[1,12,1152]{2,0,1:T(1,128)} %param.10) | copy-start | bytes 165892
  32.5 27.1 %slice-start = ((s8[5308416]{0:T(1024)(128)(4,1)}), s8[4194304]{0:T(1024)(128)(4,1)S(1)}, s32[]{:S(2)}) async-start(s8[5308416]{0:T(1024)(128)(4,1)} %bitcast.95), calls=%async_computation.1 | async-start | bytes 8388608 | tf_op jit(solution)/shard_map/cond
  32.8 26.8 %slice-start.1 = ((s8[5308416]{0:T(1024)(128)(4,1)}), s8[1114112]{0:T(1024)(128)(4,1)S(1)}, s32[]{:S(2)}) async-start(s8[5308416]{0:T(1024)(128)(4,1)} %bitcast.95), calls=%async_computation.2 | async-start | bytes 2228224 | tf_op jit(solution)/shard_map/cond
  119.4 10.4 %copy-start.5 = (f32[8]{0:T(128)S(1)}, f32[8]{0:T(128)}, u32[]{:S(2)}) copy-start(f32[8]{0:T(128)} %param.11) | copy-start | bytes 100
  126.0 18.4 %all-to-all-start = ((f32[8,1,15552]{2,1,0:T(1,128)}), f32[8,1,15552]{2,1,0:T(1,128)S(1)}, u32[]{:S(2)}, u32[]{:S(2)}) async-start(f32[8,1,15552]{2,1,0:T(1,128)} %reshape.448), calls=%async_computation | async-start | bytes 999424 | tf_op jit(solution)/shard_map/all_to_all | solution.py:149
  131.1 76.1 %copy-start.4 = (f32[8]{0:T(128)}, f32[8]{0:T(128)S(1)}, u32[]{:S(2)}) copy-start(f32[8]{0:T(128)S(1)} %broadcast_divide_fusion) | copy-start | bytes 100
  204.6 23.6 %copy-start.3 = (f32[12,144]{1,0:T(8,128)}, f32[12,144]{1,0:T(8,128)S(1)}, u32[]{:S(2)}) copy-start(f32[12,144]{1,0:T(8,128)S(1)} %get-tuple-element.202) | copy-start | bytes 20740
where the time goes:
time: 239 us; the launch traced here: 235 us
  local copies, waits for them, and re-layouts  80.6 us (34%)
  matrix products  68.3 us (29%)
  other arithmetic  51.4 us (22%)
  starting transfers between devices  18.5 us (8%)
  waiting for transfers between devices  13.3 us (6%)
    all_to_all x2, local copies, waits for them, and re-layouts, local(): lax.all_to_all(packed, 'lev', split_axis=3, concat_axis=1, tiled=True)  40 us
    unnamed x26, local copies, waits for them, and re-layouts  27.2 us
    dot_general x1, matrix products, smooth(): jnp.einsum('tlrn,nc->tlrc', field, basis, precision=lax.Precision.HIGHEST)  26.8 us
    dot_general x1, matrix products, smooth(): jnp.einsum('tlrc,nc->tlrn', spectrum, basis, precision=lax.Precision.HIGH...  24.1 us
    unnamed x1, other arithmetic  19.4 us
    dot_general x1, matrix products, local(): jnp.einsum('tirc,ikrc->tkrc', col_ratios, intersection, precision=lax.Pre...  17.4 us
    all_to_all x1, waiting for transfers between devices, local(): lax.all_to_all(packed, 'lev', split_axis=3, concat_axis=1, tiled=True)  13.3 us
    concatenate x1, local copies, waits for them, and re-layouts, local(): packed = jnp.concatenate([ratios, new_thick[None]], axis=0)  9.4 us
  transfers between devices with their start and end apart: 3, of which 1 were waited for; matrix products, arithmetic and copies ran while one was open for 29% of the time, Pallas kernels for 0%

commit v1 on v0

v1 whole, which is shorter than its diff:
```python
import math

import jax
import jax.numpy as jnp
import ml_dtypes
import numpy as np
from jax import lax
from jax.experimental import pallas as pl
from jax.experimental.pallas import tpu as pltpu
from jax.sharding import PartitionSpec as P

NT = 8
NLEV = 8
NLAT = 768
NLON = 1152
ROWS = 12
LANES = 128
CHUNKS = NLON // LANES
PIECE = NLON // NLEV
TAIL = PIECE - LANES
HALO = 3
INNER = tuple(range(HALO, ROWS - HALO))
OUTER = tuple(range(HALO)) + tuple(range(ROWS - HALO, ROWS))
HALF = ROWS // 2
MSG = 64
UP_ROWS = 248
DOWN_ROWS = 256
F32 = jnp.float32
BF16 = jnp.bfloat16


def vmem():
    return pl.BlockSpec(memory_space=pltpu.VMEM)


def params(mib):
    return pltpu.CompilerParams(vmem_limit_bytes=mib * 1024 * 1024)


def shifted(x, d):
    return x if d == 0 else pltpu.roll(x, (-d) % NLON, 1)


def face_coefs(courant):
    m = jnp.abs(courant)
    k = m * (3.0 - 2.0 * m)
    return 1.0 - 0.5 * (m + k), k, 0.5 * (m - k), courant > 0.0


def flux_stencil(mass, n, k, w, positive):
    zero = jnp.zeros_like(mass)
    a, b, c = mass * n, mass * k, mass * w
    bp, cp = jnp.where(positive, b, zero), jnp.where(positive, c, zero)
    bm, cm = b - bp, c - cp
    s, t = 7.0 / 12.0, 1.0 / 12.0
    return (
        -t * cp,
        s * cp - t * a,
        s * (a + cp) - t * cm + bp,
        s * (a + cm) - t * cp + bm,
        s * cm - t * a,
        -t * cm,
    )


def divergence_stencil(faces, ahead):
    nxt = [ahead(f) for f in faces]
    return (
        [-faces[0]] + [nxt[i] - faces[i + 1] for i in range(5)] + [nxt[5]]
    )


def meridional(band, hx, cy, e_scr, base, store):
    first = (band * ROWS).astype(F32)
    ids = first + lax.broadcasted_iota(jnp.int32, (16, LANES), 0).astype(F32)
    centre = jnp.sin(math.pi * (ids + 0.5) / NLAT)[:, :1]
    face_cos = jnp.sin(math.pi * ids / NLAT)[:, :1]
    e_scr[0:16] = (7.0 / 12.0) * (hx[1:17] + hx[2:18]) - (1.0 / 12.0) * (hx[0:16] + hx[3:19])
    e_scr[16:24] = jnp.zeros((8, NLON), F32)
    c = cy[...]
    n, k, w, positive = face_coefs(c)
    cell = jnp.where(positive, hx[2:18], hx[3:19])
    far = jnp.where(positive, e_scr[0:16], e_scr[2:18])
    mass = c * face_cos * (n * e_scr[1:17] + k * cell + w * far)
    faces = flux_stencil(mass, n, k, w, positive)

    def ahead(x):
        return pltpu.roll(x, 15, 0)

    stencil = divergence_stencil(faces, ahead)
    per_centre = 1.0 / centre
    new_thick = base - (ahead(mass) - mass) * per_centre
    inverse = 1.0 / new_thick
    scale = inverse * per_centre
    for d in range(7):
        weight = -stencil[d] * scale
        if d == 3:
            weight = weight + hx[3:19] * inverse
        store[d] = weight
    store[7] = -inverse
    return new_thick


def row_of(ref, index, row):
    return jnp.broadcast_to(ref[index, row : row + 1, :], (NT, NLON))


def lane_ids(rows=NT):
    return lax.broadcasted_iota(jnp.int32, (rows, LANES), 1)


def turn(x, amount):
    amount %= LANES
    return x if amount == 0 else pltpu.roll(x, amount, 1)


def window(lanes, low, high, dest):
    if dest == 0:
        return low
    keep = lanes < LANES - TAIL * dest
    return jnp.where(keep, turn(low, -TAIL * dest), turn(high, -TAIL * dest))


def pack_message(rows, ratio_row, new_thick, msg):
    lanes = lane_ids()
    tails = [jnp.zeros((NT, LANES), F32)] * NLEV
    for v, r in enumerate(rows):
        ratio = ratio_row(r)
        part = [ratio[:, LANES * c : LANES * (c + 1)] for c in range(CHUNKS)]
        here = (lanes >= TAIL * v) & (lanes < TAIL * (v + 1))
        for dest in range(NLEV):
            msg[dest, 8 * v : 8 * v + 8, :] = window(lanes, part[dest], part[dest + 1], dest)
            tails[dest] = jnp.where(here, turn(part[dest + 1], TAIL * (v - dest)), tails[dest])
    for dest in range(NLEV):
        msg[dest, 8 * HALF : 8 * HALF + 8, :] = tails[dest]
    lanes16 = lane_ids(16)
    wide = lane_ids(1)
    base = 8 * HALF + 8
    for dest in range(NLEV):
        low = new_thick[:, LANES * dest : LANES * (dest + 1)]
        high = new_thick[:, LANES * (dest + 1) : LANES * (dest + 2)]
        main = window(lanes16, low, high, dest)
        last = jnp.ones((1, LANES), F32)
        for v, r in enumerate(rows):
            msg[dest, base + v : base + v + 1, :] = main[r : r + 1]
            here = (wide >= TAIL * v) & (wide < TAIL * (v + 1))
            last = jnp.where(here, turn(high[r : r + 1], TAIL * (v - dest)), last)
        msg[dest, base + HALF : base + HALF + 1, :] = last
        msg[dest, base + HALF + 1 : base + HALF + 2, :] = jnp.ones((1, LANES), F32)


def edge_kernel(q_ref, h_ref, cy_ref, up_ref, down_ref):
    for ref, first in ((up_ref, ROWS - HALO), (down_ref, 0)):
        for i in range(HALO):
            row = q_ref[:, 0, first + i, :]
            for c in range(CHUNKS):
                at = 8 * (CHUNKS * i + c)
                ref[at : at + 8, :] = row[:, LANES * c : LANES * (c + 1)]
        for c in range(CHUNKS):
            at = 8 * CHUNKS * HALO + HALO * c
            ref[at : at + HALO, :] = h_ref[0, first : first + HALO, LANES * c : LANES * (c + 1)]
    for c in range(CHUNKS):
        at = (8 * HALO + HALO) * CHUNKS + c
        down_ref[at : at + 1, :] = cy_ref[0, 0:1, LANES * c : LANES * (c + 1)]
    up_ref[UP_ROWS - 5 :, :] = jnp.zeros((5, LANES), F32)
    down_ref[DOWN_ROWS - 4 :, :] = jnp.zeros((4, LANES), F32)


def split_bf16(x):
    high = x.astype(BF16)
    return high, (x - high.astype(F32)).astype(BF16)


def dot_parts(x, basis_high, basis_low, dims):
    high, low = split_bf16(x)
    rows = x.shape[0]
    both = lax.dot_general(
        jnp.concatenate([high, low], axis=0), basis_high, dims, preferred_element_type=F32
    )
    small = lax.dot_general(high, basis_low, dims, preferred_element_type=F32)
    return both[:rows] + both[rows:] + small


FORWARD = (((1,), (0,)), ((), ()))
BACKWARD = (((1,), (1,)), ((), ()))


def filter_tables():
    b = np.arange(LANES)
    m = np.arange(LANES)
    blocks = []
    for s in range(1, 5):
        angle = 2.0 * np.pi * ((b[:, None] * (CHUNKS * m[None] + s)) % NLON) / NLON
        cos, sin = np.cos(angle), np.sin(angle)
        blocks.append(np.block([[cos, -sin], [sin, cos]]))
    angle = 2.0 * np.pi * ((b[:, None] * m[None]) % LANES) / LANES
    zero = np.where(m[None] <= LANES // 2, np.cos(angle), np.sin(angle))
    wide = np.stack(blocks)

    def halves(x):
        high = x.astype(np.float32).astype(ml_dtypes.bfloat16)
        low = (x - high.astype(np.float64)).astype(np.float32).astype(ml_dtypes.bfloat16)
        return np.stack([high, low])

    waves = np.concatenate([CHUNKS * m + s for s in range(5)])
    sines = np.sin(np.pi * waves / NLON)
    limit = np.where(waves == 0, 1e30, 4.0 / np.where(waves == 0, 1.0, sines * sines))
    weight = np.full(waves.shape, 2.0 / NLON)
    weight[0] = 1.0 / NLON
    weight[LANES // 2] = 1.0 / NLON
    table = np.zeros((8, waves.size), np.float32)
    table[0], table[1] = limit, weight
    return halves(wide), halves(zero), table


def smooth(band, z_scr, spec_scr, wide_ref, zero_ref, table_ref):
    first = (band * ROWS).astype(F32)
    ids = first + lax.broadcasted_iota(jnp.int32, (16, LANES), 0).astype(F32)
    centre = jnp.sin(math.pi * (ids + 0.5) / NLAT)[:, :1]
    damping = jnp.minimum(1.0, centre * centre * table_ref[0:1, :]) * table_ref[1:2, :]
    cells = ROWS * NT
    x = [z_scr[:, LANES * a : LANES * (a + 1)] for a in range(CHUNKS)]
    plus = [x[a] + x[CHUNKS - a] for a in range(1, 5)]
    minus = [x[a] - x[CHUNKS - a] for a in range(1, 5)]

    def damp(block):
        rows = [
            jnp.broadcast_to(damping[r : r + 1, LANES * block : LANES * (block + 1)], (NT, LANES))
            for r in range(ROWS)
        ]
        return jnp.concatenate(rows, axis=0)

    total = x[0] + plus[0] + plus[1] + plus[2] + plus[3]
    spectrum = dot_parts(total, zero_ref[0], zero_ref[1], FORWARD) * damp(0)
    spec_scr[:, 0:LANES] = dot_parts(spectrum, zero_ref[0], zero_ref[1], BACKWARD)
    for s in range(1, 5):
        real, imag = x[0], None
        for a in range(1, 5):
            angle = 2.0 * math.pi * (s * a % CHUNKS) / CHUNKS
            real = real + plus[a - 1] * math.cos(angle)
            term = minus[a - 1] * -math.sin(angle)
            imag = term if imag is None else imag + term
        spectrum = dot_parts(
            jnp.concatenate([real, imag], axis=1), wide_ref[0, s - 1], wide_ref[1, s - 1], FORWARD
        )
        factor = damp(s)
        spectrum = spectrum * jnp.concatenate([factor, factor], axis=1)
        at = LANES * (2 * s - 1)
        spec_scr[:, at : at + 2 * LANES] = dot_parts(
            spectrum, wide_ref[0, s - 1], wide_ref[1, s - 1], BACKWARD
        )
    mean = spec_scr[:, 0:LANES]
    real = [spec_scr[:, LANES * (2 * s - 1) : LANES * 2 * s] for s in range(1, 5)]
    imag = [spec_scr[:, LANES * 2 * s : LANES * (2 * s + 1)] for s in range(1, 5)]
    z_scr[:, 0:LANES] = mean + real[0] + real[1] + real[2] + real[3]
    for a in range(1, 5):
        even, odd = mean, None
        for s in range(1, 5):
            angle = 2.0 * math.pi * (s * a % CHUNKS) / CHUNKS
            even = even + real[s - 1] * math.cos(angle)
            term = imag[s - 1] * math.sin(angle)
            odd = term if odd is None else odd + term
        z_scr[:, LANES * a : LANES * (a + 1)] = even - odd
        b = CHUNKS - a
        z_scr[:, LANES * b : LANES * (b + 1)] = even + odd


def combine(r, weights, q_of, z_row):
    total = row_of(weights, 7, r) * z_row
    for d in range(7):
        total = total + row_of(weights, d, r) * q_of(r + d - HALO)
    return total


def inner_kernel(
    q_in, h_in, cx_in, cy_in, wide_ref, zero_ref, table_ref,
    msg, q_out, z_out, base_out,
    cx_scr, hx_scr, cy_scr, e_scr, wx_scr, wy_scr, z_scr, spec_scr,
):
    band = lax.axis_index("lat")
    blank = jnp.zeros((4, NLON), F32)
    hx_scr[...] = jnp.zeros(hx_scr.shape, F32)
    hx_scr[HALO : HALO + ROWS] = h_in[0]
    cx_scr[0:ROWS] = cx_in[0]
    cx_scr[ROWS:16] = blank
    cy_scr[0:ROWS] = cy_in[0]
    cy_scr[ROWS:16] = blank
    h = hx_scr[HALO : HALO + 16]
    c = cx_scr[...]
    n, k, w, positive = face_coefs(c)
    west = shifted(h, -1)
    edge = (7.0 / 12.0) * (west + h) - (1.0 / 12.0) * (shifted(h, -2) + shifted(h, 1))
    far = jnp.where(positive, shifted(edge, -1), shifted(edge, 1))
    mass = c * (n * edge + k * jnp.where(positive, west, h) + w * far)
    base = h - (shifted(mass, 1) - mass)
    faces = flux_stencil(mass, n, k, w, positive)
    stencil = divergence_stencil(faces, lambda f: shifted(f, 1))
    for d in range(7):
        wx_scr[d] = stencil[d]
    base_out[...] = base
    for r in range(ROWS):
        row = q_in[:, 0, r, :]
        q_out[r] = row
        total = row_of(wx_scr, 3, r) * row
        for d in (-3, -2, -1, 1, 2, 3):
            total = total + row_of(wx_scr, d + 3, r) * shifted(row, d)
        z_scr[NT * r : NT * (r + 1), :] = total

    south, north = band * ROWS, NLAT - 1 - (band * ROWS + ROWS - 1)

    @pl.when(jnp.minimum(south, north) < NLAT // 6)
    def _():
        smooth(band, z_scr, spec_scr, wide_ref, zero_ref, table_ref)

    new_thick = meridional(band, hx_scr, cy_scr, e_scr, base, wy_scr)

    def ratio_row(r):
        return combine(r, wy_scr, lambda j: q_out[j], z_scr[NT * r : NT * (r + 1), :])

    pack_message(INNER, ratio_row, new_thick, msg)
    for v, r in enumerate(OUTER):
        z_out[v] = z_scr[NT * r : NT * (r + 1), :]


def outer_kernel(
    q_ref, z_ref, base_ref, h_in, cy_in, south_ref, north_ref,
    msg,
    hx_scr, cy_scr, e_scr, wy_scr,
):
    band = lax.axis_index("lat")
    hx_scr[HALO : HALO + ROWS] = h_in[0]
    hx_scr[ROWS + 2 * HALO : 24] = jnp.zeros((24 - ROWS - 2 * HALO, NLON), F32)
    cy_scr[0:ROWS] = cy_in[0]
    cy_scr[ROWS:16] = jnp.zeros((4, NLON), F32)
    for c in range(CHUNKS):
        at = 8 * CHUNKS * HALO + HALO * c
        lanes = slice(LANES * c, LANES * (c + 1))
        hx_scr[0:HALO, lanes] = south_ref[at : at + HALO, :]
        hx_scr[HALO + ROWS : ROWS + 2 * HALO, lanes] = north_ref[at : at + HALO, :]
        at = (8 * HALO + HALO) * CHUNKS + c
        cy_scr[ROWS : ROWS + 1, lanes] = north_ref[at : at + 1, :]
    new_thick = meridional(band, hx_scr, cy_scr, e_scr, base_ref[...], wy_scr)

    def tile_row(ref, i):
        at = 8 * CHUNKS * i
        return jnp.concatenate(
            [ref[at + 8 * c : at + 8 * c + 8, :] for c in range(CHUNKS)], axis=1
        )

    def q_of(j):
        if j < 0:
            return tile_row(south_ref, j + HALO)
        if j >= ROWS:
            return tile_row(north_ref, j - ROWS)
        return q_ref[j]

    def ratio_row(r):
        return combine(r, wy_scr, q_of, z_ref[OUTER.index(r)])

    pack_message(OUTER, ratio_row, new_thick, msg)


def remap_kernel(weight_ref, first_ref, second_ref, out_ref, mass_ref, inter_scr, main_scr, tail_scr):
    weight_sum = weight_ref[0]
    for k in range(1, NLEV):
        weight_sum = weight_sum + weight_ref[k]
    lanes = lane_ids()
    base = 8 * HALF + 8
    for in_ref, rows in ((first_ref, INNER), (second_ref, OUTER)):
        thick = [in_ref[i, base : base + 8, :] for i in range(NLEV)]
        upper, lower = [thick[0]], []
        for i in range(1, NLEV):
            upper.append(upper[-1] + thick[i])
        for i in range(NLEV):
            lower.append(upper[i] - thick[i])
        total = upper[-1]
        for v, r in enumerate(rows):
            mass_ref[r : r + 1, 0:LANES] = total[v : v + 1]
            mass_ref[r : r + 1, LANES:PIECE] = turn(total[HALF : HALF + 1], -TAIL * v)[:, :TAIL]
        reach = None
        for k in range(NLEV):
            target = total * (weight_ref[k] / weight_sum)
            reach = target if reach is None else reach + target
            start = reach - target
            scale = 1.0 / target
            for i in range(NLEV):
                overlap = jnp.minimum(upper[i], reach) - jnp.maximum(lower[i], start)
                inter_scr[NLEV * k + i] = jnp.maximum(overlap, 0.0) * scale
        for v in range(HALF + 1):
            ratio = [in_ref[i, 8 * v : 8 * v + 8, :] for i in range(NLEV)]
            for k in range(NLEV):
                moved = None
                for i in range(NLEV):
                    share = jnp.broadcast_to(inter_scr[NLEV * k + i, v : v + 1, :], (NT, LANES))
                    term = ratio[i] * share
                    moved = term if moved is None else moved + term
                if v < HALF:
                    main_scr[k, rows[v]] = moved
                else:
                    for u, r in enumerate(rows):
                        tail_scr[k, r] = turn(moved, -TAIL * u)
    for k in range(NLEV):
        main = jnp.swapaxes(main_scr[k], 0, 1)
        tail = jnp.swapaxes(tail_scr[k], 0, 1)
        out_ref[:, k, :, 0:LANES] = main[:, 0:ROWS, :]
        out_ref[:, k, :, LANES:PIECE] = tail[:, 0:ROWS, 0:TAIL]


def shape(*dims):
    return jax.ShapeDtypeStruct(dims, F32)


def scratch(*dims):
    return pltpu.VMEM(dims, F32)


def local(tracers, thickness, courant_x, courant_y, level_weights):
    bands = lax.axis_size("lat")
    wide, zero, table = filter_tables()
    up, down = pl.pallas_call(
        edge_kernel,
        out_shape=(shape(UP_ROWS, LANES), shape(DOWN_ROWS, LANES)),
        in_specs=[vmem()] * 3,
        out_specs=(vmem(),) * 2,
        compiler_params=params(16),
        name="edge_rows",
    )(tracers, thickness, courant_y)
    south = lax.ppermute(up, "lat", [(i, i + 1) for i in range(bands - 1)])
    north = lax.ppermute(down, "lat", [(i + 1, i) for i in range(bands - 1)])
    first, q, z, base = pl.pallas_call(
        inner_kernel,
        out_shape=(
            shape(NLEV, MSG, LANES), shape(ROWS, NT, NLON), shape(HALF, NT, NLON), shape(16, NLON),
        ),
        in_specs=[vmem()] * 7,
        out_specs=(vmem(),) * 4,
        scratch_shapes=[
            scratch(16, NLON), scratch(24, NLON), scratch(16, NLON), scratch(24, NLON),
            scratch(7, 16, NLON), scratch(8, 16, NLON),
            scratch(ROWS * NT, NLON), scratch(ROWS * NT, NLON),
        ],
        compiler_params=params(32),
        name="inner_rows",
    )(tracers, thickness, courant_x, courant_y, jnp.asarray(wide), jnp.asarray(zero), jnp.asarray(table))
    first = lax.all_to_all(first, "lev", split_axis=0, concat_axis=0, tiled=True)
    second = pl.pallas_call(
        outer_kernel,
        out_shape=shape(NLEV, MSG, LANES),
        in_specs=[vmem()] * 7,
        out_specs=vmem(),
        scratch_shapes=[
            scratch(24, NLON), scratch(16, NLON), scratch(24, NLON), scratch(8, 16, NLON),
        ],
        compiler_params=params(32),
        name="outer_rows",
    )(q, z, base, thickness, courant_y, south, north)
    second = lax.all_to_all(second, "lev", split_axis=0, concat_axis=0, tiled=True)
    remapped, column_mass = pl.pallas_call(
        remap_kernel,
        out_shape=(shape(NT, NLEV, ROWS, PIECE), shape(ROWS, PIECE)),
        in_specs=[pl.BlockSpec(memory_space=pltpu.SMEM), vmem(), vmem()],
        out_specs=(vmem(),) * 2,
        scratch_shapes=[scratch(NLEV * NLEV, 8, LANES), scratch(NLEV, 16, NT, LANES), scratch(NLEV, 16, NT, LANES)],
        compiler_params=params(32),
        name="remap",
    )(level_weights, first, second)
    return remapped, column_mass


def solution(mesh):
    placed = (
        P(None, "lev", "lat", None),
        P("lev", "lat", None),
        P("lev", "lat", None),
        P("lev", "lat", None),
        P(),
    )
    return jax.shard_map(
        local,
        mesh=mesh,
        in_specs=placed,
        out_specs=(P(None, None, "lat", "lev"), P("lat", "lev")),
        check_vma=False,
    )
```

time: 239 us -> 66.8 us (0.28)
  the two profiles are of different devices: /device:TPU:30 before, /device:TPU:6 now
where the time goes in v1:
time: 66.8 us; the launch traced here: 66.4 us
  blocking collectives  21.9 us (33%)
  starting transfers between devices  20.8 us (31%)
  waiting for transfers between devices  12.7 us (19%)
  Pallas kernels  5.31 us (8%)
  local copies, waits for them, and re-layouts  4.96 us (7%)
  between operations  0.73 us (1%)
    all_to_all x1, blocking collectives, local(): lax.all_to_all(second, 'lev', split_axis=0, concat_axis=0, tiled=True)  21.9 us
    ppermute x1, starting transfers between devices, local(): north = lax.ppermute(down, 'lat', [(i + 1, i) for i in range(bands - 1)])  13 us
    ppermute x1, waiting for transfers between devices, local(): south = lax.ppermute(up, 'lat', [(i, i + 1) for i in range(bands - 1)])  12.7 us
    all_to_all x1, starting transfers between devices, local(): lax.all_to_all(first, 'lev', split_axis=0, concat_axis=0, tiled=True)  5.9 us
    unnamed x14, local copies, waits for them, and re-layouts  3.63 us
    pallas_call x1, Pallas kernels, local(): pl.pallas_call(inner_kernel, out_shape=(shape(NLEV, MSG, LANES), shape(RO...  2.64 us
    ppermute x1, starting transfers between devices, local(): south = lax.ppermute(up, 'lat', [(i, i + 1) for i in range(bands - 1)])  1.92 us
    pallas_call x1, Pallas kernels, local(): pl.pallas_call(remap_kernel, out_shape=(shape(NT, NLEV, ROWS, PIECE), sha...  1.85 us
  transfers between devices with their start and end apart: 3, of which 1 were waited for; matrix products, arithmetic and copies ran while one was open for 0% of the time, Pallas kernels for 1%

profile of v1, /device:TPU:6, one launch (start us, length us, event | category | flops | bytes accessed | tf_op | source)
XLA Modules:
  0.0 66.4 jit_solution(18353094526073219492)
XLA Ops:
  0.6 0.0 copy-start
  0.6 0.9 %copy.11.h_in.h_ref = f32[1,12,1152]{2,1,0:T(8,128)S(1)} copy(f32[1,12,1152]{2,0,1:T(1,128)} %param.9) | data formatting | bytes 110592 | tf_op args[1]
  1.6 0.8 %copy.13.cy_in.cy_ref = f32[1,12,1152]{2,1,0:T(8,128)S(1)} copy(f32[1,12,1152]{2,0,1:T(1,128)} %param.11) | data formatting | bytes 110592 | tf_op args[3]
  2.4 1.1 %copy.10.q_in.q_ref = f32[8,1,12,1152]{3,2,1,0:T(8,128)S(1)} copy(f32[8,1,12,1152]{3,1,2,0:T(1,128)} %param.8) | data formatting | bytes 884736 | tf_op args[0]
  3.4 0.0 copy-done.4
  3.5 0.0 copy-start.1
  3.5 0.0 copy-start.2
  3.5 0.0 copy-done
  3.5 0.8 %copy-done.1 = bf16[2,128,128]{2,1,0:T(8,128)(2,1)S(1)} copy-done((bf16[2,128,128]{2,1,0:T(8,128)(2,1)S(1)}, bf16[2,128,128]{2,1,0:T(8,128)(2,1)}, u32[]{:S(2)}) %copy-start.1) | copy-done | bytes 65560
  4.3 0.0 copy-done.2
  4.3 2.6 %inner_rows.1 = (f32[8,64,128]{2,1,0:T(8,128)}, f32[12,8,1152]{2,1,0:T(8,128)S(1)}, f32[6,8,1152]{2,1,0:T(8,128)S(1)}, f32[16,1152]{1,0:T(8,128)S(1)}) custom-call(f32[8,1,12,1152]{3,2,1,0:T(8,128)S(1)} %copy.10.q_in.q_ref, f32[1,12,1152]{2,1,0:T(8,128)S(1)} %copy.11.h_in.h_ref, f32[1,12,1152]{2,1,0:T(8,128)S(1)} %copy.12.cx_in, ...), custom_call_target="tpu_custom_call" | custom-call | tf_op jit(solution)/shard_map/inner_rows/pallas_call | solution.py:430
  6.9 5.9 %all-to-all-start = ((f32[8,64,128]{2,1,0:T(8,128)}), f32[8,64,128]{2,1,0:T(8,128)S(1)}, u32[]{:S(2)}, u32[]{:S(2)}) async-start(f32[8,64,128]{2,1,0:T(8,128)} %get-tuple-element.8), calls=%async_computation | async-start | bytes 524288 | tf_op jit(solution)/shard_map/all_to_all | solution.py:445
  12.8 0.1 edge_rows.1
  12.9 13.0 %collective-permute-start.1 = (f32[256,128]{1,0:T(8,128)S(1)}, f32[256,128]{1,0:T(8,128)S(1)}, u32[]{:S(2)}, u32[]{:S(2)}) collective-permute-start(f32[256,128]{1,0:T(8,128)S(1)} %get-tuple-element.13), channel_id=1, source_target_pairs={{8,0},{16,8},{24,16},{32,24},{40,32},{48,40},{56,48},{64,56},{72,6... | collective-permute-start | bytes 393224 | tf_op jit(solution)/shard_map/ppermute | solution.py:429
  25.9 1.9 %collective-permute-start = (f32[248,128]{1,0:T(8,128)S(1)}, f32[248,128]{1,0:T(8,128)S(1)}, u32[]{:S(2)}, u32[]{:S(2)}) collective-permute-start(f32[248,128]{1,0:T(8,128)S(1)} %get-tuple-element.12), channel_id=1, source_target_pairs={{0,8},{8,16},{16,24},{24,32},{32,40},{40,48},{48,56},{56,64},{64,7... | collective-permute-start | bytes 380936 | tf_op jit(solution)/shard_map/ppermute | solution.py:428
  27.8 12.7 %collective-permute-done.south_ref = f32[248,128]{1,0:T(8,128)S(1)} collective-permute-done((f32[248,128]{1,0:T(8,128)S(1)}, f32[248,128]{1,0:T(8,128)S(1)}, u32[]{:S(2)}, u32[]{:S(2)}) %collective-permute-start) | collective-permute-done | bytes 127008 | tf_op jit(solution)/shard_map/ppermute | solution.py:428
  40.5 0.0 collective-permute-done.1.north_ref
  40.5 0.8 %outer_rows.1 = f32[8,64,128]{2,1,0:T(8,128)S(1)} custom-call(f32[12,8,1152]{2,1,0:T(8,128)S(1)} %get-tuple-element.9.q_ref, f32[6,8,1152]{2,1,0:T(8,128)S(1)} %get-tuple-element.10.z_ref, f32[16,1152]{1,0:T(8,128)S(1)} %get-tuple-element.11.base_ref, f32[1,12,1152]{2,1,0:T(8,128)S(1)} %copy.11.h_in.h_ref, f32[1,12,1152]{2,1,0:T(8,128)S(1)} %copy.13.cy_in.cy_ref, ...), custom_call_target="tpu_custom_call" | custom-call | tf_op jit(solution)/shard_map/outer_rows/pallas_call | solution.py:446
  41.2 0.0 copy-start.3
  41.3 0.0 all-to-all-done.first_ref
  41.3 21.9 %all_to_all.10.second_ref = f32[8,64,128]{2,1,0:T(8,128)S(1)} all-to-all(f32[8,64,128]{2,1,0:T(8,128)S(1)} %outer_rows.1), channel_id=1, replica_groups=mesh['lat'=64,'lev'=8] {'lev'}, dimensions={0} | all-to-all | bytes 524288 | tf_op jit(solution)/shard_map/all_to_all | solution.py:457
  63.2 0.0 copy-done.3
  63.2 1.8 %remap.1 = (f32[8,8,12,144]{3,2,1,0:T(8,128)S(1)}, f32[12,144]{1,0:T(8,128)}) custom-call(f32[8]{0:T(128)S(1)} %copy-done.3, f32[8,64,128]{2,1,0:T(8,128)S(1)} %all-to-all-done.first_ref, f32[8,64,128]{2,1,0:T(8,128)S(1)} %all_to_all.10.second_ref), custom_call_target="tpu_custom_call" | custom-call | tf_op jit(solution)/shard_map/remap/pallas_call | solution.py:458
  65.1 1.3 %copy.19 = f32[8,8,12,144]{3,1,2,0:T(8,128)} copy(f32[8,8,12,144]{3,2,1,0:T(8,128)S(1)} %get-tuple-element.14) | data formatting | bytes 884736 | tf_op jit(solution)/shard_map/remap/pallas_call | solution.py:458
  (2 shorter events, 0.0 us)
Async XLA Ops:
  0.6 2.9 %copy-start = (bf16[2,4,256,256]{3,2,1,0:T(8,128)(2,1)S(1)}, bf16[2,4,256,256]{3,2,1,0:T(8,128)(2,1)}, u32[]{:S(2)}) copy-start(bf16[2,4,256,256]{3,2,1,0:T(8,128)(2,1)} %constant.6.clone.wide_ref) | copy-start | bytes 3145732
  2.4 1.1 %copy-start.4 = (f32[1,12,1152]{2,0,1:T(1,128)S(1)}, f32[1,12,1152]{2,0,1:T(1,128)}, u32[]{:S(2)}) copy-start(f32[1,12,1152]{2,0,1:T(1,128)} %param.10) | copy-start | bytes 165892
  3.5 0.8 %copy-start.1 = (bf16[2,128,128]{2,1,0:T(8,128)(2,1)S(1)}, bf16[2,128,128]{2,1,0:T(8,128)(2,1)}, u32[]{:S(2)}) copy-start(bf16[2,128,128]{2,1,0:T(8,128)(2,1)} %constant.7.clone.zero_ref) | copy-start | bytes 196612
  3.5 0.8 %copy-start.2 = (f32[8,640]{1,0:T(8,128)S(1)}, f32[8,640]{1,0:T(8,128)}, u32[]{:S(2)}) copy-start(f32[8,640]{1,0:T(8,128)} %constant.8.clone.table_ref) | copy-start | bytes 61444
  6.9 34.3 %all-to-all-start = ((f32[8,64,128]{2,1,0:T(8,128)}), f32[8,64,128]{2,1,0:T(8,128)S(1)}, u32[]{:S(2)}, u32[]{:S(2)}) async-start(f32[8,64,128]{2,1,0:T(8,128)} %get-tuple-element.8), calls=%async_computation | async-start | bytes 524288 | tf_op jit(solution)/shard_map/all_to_all | solution.py:445
  12.9 27.6 %collective-permute-start.1 = (f32[256,128]{1,0:T(8,128)S(1)}, f32[256,128]{1,0:T(8,128)S(1)}, u32[]{:S(2)}, u32[]{:S(2)}) collective-permute-start(f32[256,128]{1,0:T(8,128)S(1)} %get-tuple-element.13), channel_id=1, source_target_pairs={{8,0},{16,8},{24,16},{32,24},{40,32},{48,40},{56,48},{64,56},{72,6... | collective-permute-start | bytes 393224 | tf_op jit(solution)/shard_map/ppermute | solution.py:429
  25.9 14.6 %collective-permute-start = (f32[248,128]{1,0:T(8,128)S(1)}, f32[248,128]{1,0:T(8,128)S(1)}, u32[]{:S(2)}, u32[]{:S(2)}) collective-permute-start(f32[248,128]{1,0:T(8,128)S(1)} %get-tuple-element.12), channel_id=1, source_target_pairs={{0,8},{8,16},{16,24},{24,32},{32,40},{40,48},{48,56},{56,64},{64,7... | collective-permute-start | bytes 380936 | tf_op jit(solution)/shard_map/ppermute | solution.py:428
  41.2 22.0 %copy-start.3 = (f32[8]{0:T(128)S(1)}, f32[8]{0:T(128)}, u32[]{:S(2)}) copy-start(f32[8]{0:T(128)} %weight_ref.1) | copy-start | bytes 100

commit v2 on v1

--- a/solution.py
+++ b/solution.py
@@ -23,14 +23,27 @@
 OUTER = tuple(range(HALO)) + tuple(range(ROWS - HALO, ROWS))
 HALF = ROWS // 2
 MSG = 64
-UP_ROWS = 248
-DOWN_ROWS = 256
+SEND = 256
+ZFLOPS = 2 * 10**10
+ZBYTES = 10**10
+WHOLE = 62
 F32 = jnp.float32
 BF16 = jnp.bfloat16
 
 
 def vmem():
     return pl.BlockSpec(memory_space=pltpu.VMEM)
+
+
+def far():
+    return pl.BlockSpec(memory_space=pltpu.HBM)
+
+
+def copies(semaphores, *pairs):
+    return [
+        pltpu.make_async_copy(source, target, semaphores.at[i])
+        for i, (source, target) in enumerate(pairs)
+    ]
 
 
 def params(mib):
@@ -149,21 +162,44 @@
         msg[dest, base + HALF + 1 : base + HALF + 2, :] = jnp.ones((1, LANES), F32)
 
 
-def edge_kernel(q_ref, h_ref, cy_ref, up_ref, down_ref):
-    for ref, first in ((up_ref, ROWS - HALO), (down_ref, 0)):
+def tracer_tile(ref, row, chunk):
+    return ref[pl.ds(CHUNKS * row + chunk, NT, stride=CHUNKS * ROWS), :]
+
+
+def edge_kernel(
+    q_in, h_in, cy_in,
+    odd_ref, even_ref,
+    q_ref, h_ref, cy_ref, semaphores,
+):
+    band = lax.axis_index("lat")
+    loads = copies(semaphores, (q_in, q_ref), (h_in, h_ref), (cy_in, cy_ref))
+    for load in loads:
+        load.start()
+    for load in loads:
+        load.wait()
+
+    def put(ref, first):
         for i in range(HALO):
-            row = q_ref[:, 0, first + i, :]
             for c in range(CHUNKS):
                 at = 8 * (CHUNKS * i + c)
-                ref[at : at + 8, :] = row[:, LANES * c : LANES * (c + 1)]
-        for c in range(CHUNKS):
-            at = 8 * CHUNKS * HALO + HALO * c
-            ref[at : at + HALO, :] = h_ref[0, first : first + HALO, LANES * c : LANES * (c + 1)]
-    for c in range(CHUNKS):
-        at = (8 * HALO + HALO) * CHUNKS + c
-        down_ref[at : at + 1, :] = cy_ref[0, 0:1, LANES * c : LANES * (c + 1)]
-    up_ref[UP_ROWS - 5 :, :] = jnp.zeros((5, LANES), F32)
-    down_ref[DOWN_ROWS - 4 :, :] = jnp.zeros((4, LANES), F32)
+                ref[at : at + 8, :] = tracer_tile(q_ref, first + i, c)
+        at = 8 * CHUNKS * HALO
+        size = CHUNKS * HALO
+        for i in range(size):
+            ref[at + i : at + i + 1, :] = h_ref[CHUNKS * first + i]
+        for i in range(CHUNKS):
+            ref[at + size + i : at + size + i + 1, :] = cy_ref[i]
+        ref[at + size + CHUNKS : SEND, :] = jnp.zeros((SEND - at - size - CHUNKS, LANES), F32)
+
+    @pl.when(band % 2 == 0)
+    def _():
+        put(even_ref, ROWS - HALO)
+        put(odd_ref, 0)
+
+    @pl.when(band % 2 == 1)
+    def _():
+        put(odd_ref, ROWS - HALO)
+        put(even_ref, 0)
 
 
 def split_bf16(x):
@@ -213,22 +249,21 @@
     return halves(wide), halves(zero), table
 
 
-def smooth(band, z_scr, spec_scr, wide_ref, zero_ref, table_ref):
+def smooth(band, rows, z_scr, spec_scr, wide_ref, zero_ref, table_ref):
     first = (band * ROWS).astype(F32)
     ids = first + lax.broadcasted_iota(jnp.int32, (16, LANES), 0).astype(F32)
     centre = jnp.sin(math.pi * (ids + 0.5) / NLAT)[:, :1]
     damping = jnp.minimum(1.0, centre * centre * table_ref[0:1, :]) * table_ref[1:2, :]
-    cells = ROWS * NT
     x = [z_scr[:, LANES * a : LANES * (a + 1)] for a in range(CHUNKS)]
     plus = [x[a] + x[CHUNKS - a] for a in range(1, 5)]
     minus = [x[a] - x[CHUNKS - a] for a in range(1, 5)]
 
     def damp(block):
-        rows = [
+        blocks = [
             jnp.broadcast_to(damping[r : r + 1, LANES * block : LANES * (block + 1)], (NT, LANES))
-            for r in range(ROWS)
+            for r in rows
         ]
-        return jnp.concatenate(rows, axis=0)
+        return jnp.concatenate(blocks, axis=0)
 
     total = x[0] + plus[0] + plus[1] + plus[2] + plus[3]
     spectrum = dot_parts(total, zero_ref[0], zero_ref[1], FORWARD) * damp(0)
@@ -272,19 +307,23 @@
     return total
 
 
-def inner_kernel(
-    q_in, h_in, cx_in, cy_in, wide_ref, zero_ref, table_ref,
-    msg, q_out, z_out, base_out,
-    cx_scr, hx_scr, cy_scr, e_scr, wx_scr, wy_scr, z_scr, spec_scr,
-):
+def spread(ref, scr, at):
+    for r in range(ROWS):
+        for c in range(CHUNKS):
+            scr[at + r : at + r + 1, LANES * c : LANES * (c + 1)] = ref[CHUNKS * r + c]
+
+
+def is_polar(band):
+    south, north = band * ROWS, NLAT - 1 - (band * ROWS + ROWS - 1)
+    return jnp.minimum(south, north) < NLAT // 6
+
+
+def zonal(rows, q_in, h_in, cx_in, cx_scr, hx_scr, wx_scr, z_scr, smooth_rows):
     band = lax.axis_index("lat")
-    blank = jnp.zeros((4, NLON), F32)
     hx_scr[...] = jnp.zeros(hx_scr.shape, F32)
-    hx_scr[HALO : HALO + ROWS] = h_in[0]
-    cx_scr[0:ROWS] = cx_in[0]
-    cx_scr[ROWS:16] = blank
-    cy_scr[0:ROWS] = cy_in[0]
-    cy_scr[ROWS:16] = blank
+    spread(h_in, hx_scr, HALO)
+    spread(cx_in, cx_scr, 0)
+    cx_scr[ROWS:16] = jnp.zeros((4, NLON), F32)
     h = hx_scr[HALO : HALO + 16]
     c = cx_scr[...]
     n, k, w, positive = face_coefs(c)
@@ -292,79 +331,130 @@
     edge = (7.0 / 12.0) * (west + h) - (1.0 / 12.0) * (shifted(h, -2) + shifted(h, 1))
     far = jnp.where(positive, shifted(edge, -1), shifted(edge, 1))
     mass = c * (n * edge + k * jnp.where(positive, west, h) + w * far)
-    base = h - (shifted(mass, 1) - mass)
     faces = flux_stencil(mass, n, k, w, positive)
     stencil = divergence_stencil(faces, lambda f: shifted(f, 1))
     for d in range(7):
         wx_scr[d] = stencil[d]
-    base_out[...] = base
-    for r in range(ROWS):
-        row = q_in[:, 0, r, :]
-        q_out[r] = row
+    for v, r in enumerate(rows):
+        row = tracer_row(q_in, r)
         total = row_of(wx_scr, 3, r) * row
         for d in (-3, -2, -1, 1, 2, 3):
             total = total + row_of(wx_scr, d + 3, r) * shifted(row, d)
-        z_scr[NT * r : NT * (r + 1), :] = total
-
-    south, north = band * ROWS, NLAT - 1 - (band * ROWS + ROWS - 1)
-
-    @pl.when(jnp.minimum(south, north) < NLAT // 6)
+        z_scr[NT * v : NT * (v + 1), :] = total
+
+    @pl.when(is_polar(band))
     def _():
-        smooth(band, z_scr, spec_scr, wide_ref, zero_ref, table_ref)
-
-    new_thick = meridional(band, hx_scr, cy_scr, e_scr, base, wy_scr)
-
-    def ratio_row(r):
-        return combine(r, wy_scr, lambda j: q_out[j], z_scr[NT * r : NT * (r + 1), :])
-
-    pack_message(INNER, ratio_row, new_thick, msg)
-    for v, r in enumerate(OUTER):
-        z_out[v] = z_scr[NT * r : NT * (r + 1), :]
-
-
-def outer_kernel(
-    q_ref, z_ref, base_ref, h_in, cy_in, south_ref, north_ref,
+        smooth_rows(band)
+
+    return h - (shifted(mass, 1) - mass)
+
+
+def tracer_row(ref, row):
+    return jnp.concatenate([tracer_tile(ref, row, chunk) for chunk in range(CHUNKS)], axis=1)
+
+
+def inner_kernel(
+    q_far, h_far, cx_far, cy_far, wide_far, zero_far, table_far, _sent,
     msg,
-    hx_scr, cy_scr, e_scr, wy_scr,
+    cx_scr, hx_scr, cy_scr, e_scr, wx_scr, wy_scr, z_scr, spec_scr, q_scr,
+    q_in, h_in, cx_in, cy_in, wide_ref, zero_ref, table_ref, semaphores,
 ):
     band = lax.axis_index("lat")
-    hx_scr[HALO : HALO + ROWS] = h_in[0]
+    *fields, wide_load, zero_load, table_load = copies(
+        semaphores, (q_far, q_in), (h_far, h_in), (cx_far, cx_in), (cy_far, cy_in),
+        (wide_far, wide_ref), (zero_far, zero_ref), (table_far, table_ref),
+    )
+    loads = (wide_load, zero_load, table_load)
+    for load in fields:
+        load.start()
+
+    @pl.when(is_polar(band))
+    def _():
+        for load in loads:
+            load.start()
+
+    def smooth_rows(band):
+        for load in loads:
+            load.wait()
+        smooth(band, INNER, z_scr, spec_scr, wide_ref, zero_ref, table_ref)
+
+    for load in fields:
+        load.wait()
+    base = zonal(INNER, q_in, h_in, cx_in, cx_scr, hx_scr, wx_scr, z_scr, smooth_rows)
+    spread(cy_in, cy_scr, 0)
+    cy_scr[ROWS:16] = jnp.zeros((4, NLON), F32)
+    new_thick = meridional(band, hx_scr, cy_scr, e_scr, base, wy_scr)
+    for r in range(ROWS):
+        q_scr[r] = tracer_row(q_in, r)
+
+    def ratio_row(r):
+        v = INNER.index(r)
+        return combine(r, wy_scr, lambda j: q_scr[j], z_scr[NT * v : NT * (v + 1), :])
+
+    pack_message(INNER, ratio_row, new_thick, msg)
+
+
+def zonal_kernel(
+    q_in, h_in, cx_in, wide_ref, zero_ref, table_ref,
+    z_out, base_out,
+    cx_scr, hx_scr, wx_scr, spec_scr,
+):
+    def smooth_rows(band):
+        smooth(band, OUTER, z_out, spec_scr, wide_ref, zero_ref, table_ref)
+
+    base_out[...] = zonal(OUTER, q_in, h_in, cx_in, cx_scr, hx_scr, wx_scr, z_out, smooth_rows)
+
+
+def outer_kernel(
+    q_in, z_ref, base_ref, h_in, cy_in, odd_ref, even_ref,
+    msg,
+    hx_scr, cy_scr, e_scr, wy_scr, q_scr,
+):
+    band = lax.axis_index("lat")
+    spread(h_in, hx_scr, HALO)
     hx_scr[ROWS + 2 * HALO : 24] = jnp.zeros((24 - ROWS - 2 * HALO, NLON), F32)
-    cy_scr[0:ROWS] = cy_in[0]
+    spread(cy_in, cy_scr, 0)
     cy_scr[ROWS:16] = jnp.zeros((4, NLON), F32)
-    for c in range(CHUNKS):
-        at = 8 * CHUNKS * HALO + HALO * c
-        lanes = slice(LANES * c, LANES * (c + 1))
-        hx_scr[0:HALO, lanes] = south_ref[at : at + HALO, :]
-        hx_scr[HALO + ROWS : ROWS + 2 * HALO, lanes] = north_ref[at : at + HALO, :]
-        at = (8 * HALO + HALO) * CHUNKS + c
-        cy_scr[ROWS : ROWS + 1, lanes] = north_ref[at : at + 1, :]
+
+    def take(south_ref, north_ref):
+        for i in range(HALO):
+            for c in range(CHUNKS):
+                at = 8 * (CHUNKS * i + c)
+                lanes = slice(LANES * c, LANES * (c + 1))
+                q_scr[i, :, lanes] = south_ref[at : at + 8, :]
+                q_scr[HALO + ROWS + i, :, lanes] = north_ref[at : at + 8, :]
+        for c in range(CHUNKS):
+            at = 8 * CHUNKS * HALO + c
+            lanes = slice(LANES * c, LANES * (c + 1))
+            hx_scr[0:HALO, lanes] = south_ref[pl.ds(at, HALO, stride=CHUNKS), :]
+            hx_scr[HALO + ROWS : ROWS + 2 * HALO, lanes] = north_ref[pl.ds(at, HALO, stride=CHUNKS), :]
+            at = at + CHUNKS * HALO
+            cy_scr[ROWS : ROWS + 1, lanes] = north_ref[at : at + 1, :]
+
+    @pl.when(band % 2 == 0)
+    def _():
+        take(odd_ref, even_ref)
+
+    @pl.when(band % 2 == 1)
+    def _():
+        take(even_ref, odd_ref)
+
     new_thick = meridional(band, hx_scr, cy_scr, e_scr, base_ref[...], wy_scr)
 
-    def tile_row(ref, i):
-        at = 8 * CHUNKS * i
-        return jnp.concatenate(
-            [ref[at + 8 * c : at + 8 * c + 8, :] for c in range(CHUNKS)], axis=1
-        )
-
-    def q_of(j):
-        if j < 0:
-            return tile_row(south_ref, j + HALO)
-        if j >= ROWS:
-            return tile_row(north_ref, j - ROWS)
-        return q_ref[j]
+    for r in range(ROWS):
+        q_scr[HALO + r] = tracer_row(q_in, r)
 
     def ratio_row(r):
-        return combine(r, wy_scr, q_of, z_ref[OUTER.index(r)])
+        v = OUTER.index(r)
+        return combine(r, wy_scr, lambda j: q_scr[HALO + j], z_ref[NT * v : NT * (v + 1), :])
 
     pack_message(OUTER, ratio_row, new_thick, msg)
 
 
-def remap_kernel(weight_ref, first_ref, second_ref, out_ref, mass_ref, inter_scr, main_scr, tail_scr):
+def remap_kernel(weight_ref, first_ref, second_ref, out_ref, mass_ref, inter_scr):
     weight_sum = weight_ref[0]
     for k in range(1, NLEV):
         weight_sum = weight_sum + weight_ref[k]
-    lanes = lane_ids()
     base = 8 * HALF + 8
     for in_ref, rows in ((first_ref, INNER), (second_ref, OUTER)):
         thick = [in_ref[i, base : base + 8, :] for i in range(NLEV)]
@@ -385,25 +475,27 @@
             scale = 1.0 / target
             for i in range(NLEV):
                 overlap = jnp.minimum(upper[i], reach) - jnp.maximum(lower[i], start)
-                inter_scr[NLEV * k + i] = jnp.maximum(overlap, 0.0) * scale
+                at = 8 * (NLEV * i + k)
+                inter_scr[at : at + 8, :] = jnp.maximum(overlap, 0.0) * scale
         for v in range(HALF + 1):
-            ratio = [in_ref[i, 8 * v : 8 * v + 8, :] for i in range(NLEV)]
-            for k in range(NLEV):
-                moved = None
-                for i in range(NLEV):
-                    share = jnp.broadcast_to(inter_scr[NLEV * k + i, v : v + 1, :], (NT, LANES))
-                    term = ratio[i] * share
-                    moved = term if moved is None else moved + term
+            moved = [None] * NT
+            for i in range(NLEV):
+                share = inter_scr[pl.ds(8 * NLEV * i + v, NLEV, stride=8), :]
+                for t in range(NT):
+                    at = 8 * v + t
+                    term = jnp.broadcast_to(in_ref[i, at : at + 1, :], (NLEV, LANES)) * share
+                    moved[t] = term if i == 0 else moved[t] + term
+            for t in range(NT):
                 if v < HALF:
-                    main_scr[k, rows[v]] = moved
+                    out_ref[t, rows[v], :, 0:LANES] = moved[t]
                 else:
                     for u, r in enumerate(rows):
-                        tail_scr[k, r] = turn(moved, -TAIL * u)
-    for k in range(NLEV):
-        main = jnp.swapaxes(main_scr[k], 0, 1)
-        tail = jnp.swapaxes(tail_scr[k], 0, 1)
-        out_ref[:, k, :, 0:LANES] = main[:, 0:ROWS, :]
-        out_ref[:, k, :, LANES:PIECE] = tail[:, 0:ROWS, 0:TAIL]
+                        out_ref[t, r, :, LANES:PIECE] = turn(moved[t], -TAIL * u)[:, :TAIL]
+
+
+def swaps(first, bands):
+    low = range(first, bands - 1, 2)
+    return [(i, i + 1) for i in low] + [(i + 1, i) for i in low]
 
 
 def shape(*dims):
@@ -417,32 +509,56 @@
 def local(tracers, thickness, courant_x, courant_y, level_weights):
     bands = lax.axis_size("lat")
     wide, zero, table = filter_tables()
-    up, down = pl.pallas_call(
+    q_in = tracers.reshape(NT * ROWS * CHUNKS, LANES)
+    h_in, cx_in, cy_in = (
+        field.reshape(ROWS * CHUNKS, 1, LANES) for field in (thickness, courant_x, courant_y)
+    )
+    odd, even = pl.pallas_call(
         edge_kernel,
-        out_shape=(shape(UP_ROWS, LANES), shape(DOWN_ROWS, LANES)),
-        in_specs=[vmem()] * 3,
+        out_shape=(shape(SEND, LANES),) * 2,
+        in_specs=[far()] * 3,
         out_specs=(vmem(),) * 2,
-        compiler_params=params(16),
+        scratch_shapes=[
+            scratch(NT * ROWS * CHUNKS, LANES), scratch(ROWS * CHUNKS, 1, LANES),
+            scratch(ROWS * CHUNKS, 1, LANES), pltpu.SemaphoreType.DMA((3,)),
+        ],
+        compiler_params=params(WHOLE),
         name="edge_rows",
-    )(tracers, thickness, courant_y)
-    south = lax.ppermute(up, "lat", [(i, i + 1) for i in range(bands - 1)])
-    north = lax.ppermute(down, "lat", [(i + 1, i) for i in range(bands - 1)])
-    first, q, z, base = pl.pallas_call(
+    )(q_in, h_in, cy_in)
+    sent = odd
+    odd = lax.ppermute(odd, "lat", swaps(1, bands))
+    even = lax.ppermute(even, "lat", swaps(0, bands))
+    tables = (jnp.asarray(wide), jnp.asarray(zero), jnp.asarray(table))
+    first = pl.pallas_call(
         inner_kernel,
-        out_shape=(
-            shape(NLEV, MSG, LANES), shape(ROWS, NT, NLON), shape(HALF, NT, NLON), shape(16, NLON),
-        ),
-        in_specs=[vmem()] * 7,
-        out_specs=(vmem(),) * 4,
+        out_shape=shape(NLEV, MSG, LANES),
+        in_specs=[far()] * 8,
+        out_specs=vmem(),
         scratch_shapes=[
             scratch(16, NLON), scratch(24, NLON), scratch(16, NLON), scratch(24, NLON),
             scratch(7, 16, NLON), scratch(8, 16, NLON),
-            scratch(ROWS * NT, NLON), scratch(ROWS * NT, NLON),
+            scratch(HALF * NT, NLON), scratch(HALF * NT, NLON), scratch(ROWS, NT, NLON),
+            scratch(NT * ROWS * CHUNKS, LANES),
+        ]
+        + [scratch(ROWS * CHUNKS, 1, LANES)] * 3
+        + [pltpu.VMEM(t.shape, t.dtype) for t in tables]
+        + [pltpu.SemaphoreType.DMA((7,))],
+        compiler_params=params(WHOLE),
+        name="inner_rows",
+    )(q_in, h_in, cx_in, cy_in, *tables, sent)
+    first = lax.all_to_all(first, "lev", split_axis=0, concat_axis=0, tiled=True)
+    z, base = pl.pallas_call(
+        zonal_kernel,
+        out_shape=(shape(HALF * NT, NLON), shape(16, NLON)),
+        in_specs=[vmem()] * 6,
+        out_specs=(vmem(),) * 2,
+        scratch_shapes=[
+            scratch(16, NLON), scratch(24, NLON), scratch(7, 16, NLON), scratch(HALF * NT, NLON),
         ],
         compiler_params=params(32),
-        name="inner_rows",
-    )(tracers, thickness, courant_x, courant_y, jnp.asarray(wide), jnp.asarray(zero), jnp.asarray(table))
-    first = lax.all_to_all(first, "lev", split_axis=0, concat_axis=0, tiled=True)
+        cost_estimate=pl.CostEstimate(flops=ZFLOPS, bytes_accessed=ZBYTES, transcendentals=0),
+        name="outer_zonal",
+    )(q_in, h_in, cx_in, *tables)
     second = pl.pallas_call(
         outer_kernel,
         out_shape=shape(NLEV, MSG, LANES),
@@ -450,21 +566,22 @@
         out_specs=vmem(),
         scratch_shapes=[
             scratch(24, NLON), scratch(16, NLON), scratch(24, NLON), scratch(8, 16, NLON),
+            scratch(ROWS + 2 * HALO, NT, NLON),
         ],
         compiler_params=params(32),
         name="outer_rows",
-    )(q, z, base, thickness, courant_y, south, north)
+    )(q_in, z, base, h_in, cy_in, odd, even)
     second = lax.all_to_all(second, "lev", split_axis=0, concat_axis=0, tiled=True)
     remapped, column_mass = pl.pallas_call(
         remap_kernel,
-        out_shape=(shape(NT, NLEV, ROWS, PIECE), shape(ROWS, PIECE)),
+        out_shape=(shape(NT, ROWS, NLEV, PIECE), shape(ROWS, PIECE)),
         in_specs=[pl.BlockSpec(memory_space=pltpu.SMEM), vmem(), vmem()],
         out_specs=(vmem(),) * 2,
-        scratch_shapes=[scratch(NLEV * NLEV, 8, LANES), scratch(NLEV, 16, NT, LANES), scratch(NLEV, 16, NT, LANES)],
+        scratch_shapes=[scratch(NLEV * NLEV * 8, LANES)],
         compiler_params=params(32),
         name="remap",
     )(level_weights, first, second)
-    return remapped, column_mass
+    return jnp.transpose(remapped, (0, 2, 1, 3)), column_mass
 
 
 def solution(mesh):

time: 66.8 us -> 54.6 us (0.82)
  blocking collectives: 21.9 us -> 12.1 us
  waiting for transfers between devices: 12.7 us -> 7.78 us
  local copies, waits for them, and re-layouts: 4.96 us -> 0.05 us
  Pallas kernels: 5.31 us -> 9.08 us
  starting transfers between devices: 20.8 us -> 24.5 us
    all_to_all x1, blocking collectives: 21.9 us -> 12.1 us  [local(): lax.all_to_all(second, 'lev', split_axis=0, concat_axis=0, tiled=True)]
    ppermute x2, waiting for transfers between devices: 12.7 us -> 3.26 us  [the longest x1 3.26 us: local(): odd = lax.ppermute(odd, 'lat', swaps(1, bands))]
    ppermute x2, starting transfers between devices: 14.9 us -> 20.9 us  [the longest x1 11.8 us: local(): odd = lax.ppermute(odd, 'lat', swaps(1, bands))]
    all_to_all x1, waiting for transfers between devices: 0.01 us -> 4.52 us  [local(): lax.all_to_all(first, 'lev', split_axis=0, concat_axis=0, tiled=True)]
    pallas_call x3 -> x4, Pallas kernels: 4.56 us -> 8.19 us  [the longest x1 3.4 us: local(): pl.pallas_call(inner_kernel, out_shape=shape(NLEV, MSG, LANES), in_specs=...]
    unnamed x14 -> x16, local copies, waits for them, and re-layouts: 3.63 us -> 0.05 us
    all_to_all x1, starting transfers between devices: 5.9 us -> 3.56 us  [local(): lax.all_to_all(first, 'lev', split_axis=0, concat_axis=0, tiled=True)]
    pallas_call x1 -> x0, local copies, waits for them, and re-layouts: 1.34 us -> none  [local(): pl.pallas_call(remap_kernel, out_shape=(shape(NT, NLEV, ROWS, PIECE), sha...]
  transfers between devices with their start and end apart: 3 -> 3, of which waited for: 1 -> 2; matrix products, arithmetic and copies ran while one was open for 0% -> 0% of each run, Pallas kernels for 1% -> 10%
where the time goes in v2:
time: 54.6 us; the launch traced here: 54.3 us
  starting transfers between devices  24.5 us (45%)
  blocking collectives  12.1 us (22%)
  Pallas kernels  9.08 us (17%)
  waiting for transfers between devices  7.78 us (14%)
  between operations  0.81 us (1%)
    all_to_all x1, blocking collectives, local(): lax.all_to_all(second, 'lev', split_axis=0, concat_axis=0, tiled=True)  12.1 us
    ppermute x1, starting transfers between devices, local(): odd = lax.ppermute(odd, 'lat', swaps(1, bands))  11.8 us
    ppermute x1, starting transfers between devices, local(): even = lax.ppermute(even, 'lat', swaps(0, bands))  9.1 us
    all_to_all x1, waiting for transfers between devices, local(): lax.all_to_all(first, 'lev', split_axis=0, concat_axis=0, tiled=True)  4.52 us
    all_to_all x1, starting transfers between devices, local(): lax.all_to_all(first, 'lev', split_axis=0, concat_axis=0, tiled=True)  3.56 us
    pallas_call x1, Pallas kernels, local(): pl.pallas_call(inner_kernel, out_shape=shape(NLEV, MSG, LANES), in_specs=...  3.4 us
    ppermute x1, waiting for transfers between devices, local(): odd = lax.ppermute(odd, 'lat', swaps(1, bands))  3.26 us
    pallas_call x1, Pallas kernels, local(): pl.pallas_call(remap_kernel, out_shape=(shape(NT, ROWS, NLEV, PIECE), sha...  2.13 us
  transfers between devices with their start and end apart: 3, of which 2 were waited for; matrix products, arithmetic and copies ran while one was open for 0% of the time, Pallas kernels for 10%

profile of v2, /device:TPU:6, one launch (start us, length us, event | category | flops | bytes accessed | tf_op | source)
XLA Modules:
  0.0 54.3 jit_solution(1106040153169998816)
XLA Ops:
  0.6 1.8 %edge_rows.1 = (f32[256,128]{1,0:T(8,128)}, f32[256,128]{1,0:T(8,128)}) custom-call(f32[864,128]{1,0:T(8,128)} %bitcast.5, f32[108,1,128]{2,1,0:T(1,128)} %bitcast.9, f32[108,1,128]{2,1,0:T(1,128)} %bitcast.13), custom_call_target="tpu_custom_call" | custom-call | tf_op jit(solution)/shard_map/edge_rows/pallas_call | solution.py:516
  2.4 9.1 %collective-permute-start.1 = (f32[256,128]{1,0:T(8,128)}, f32[256,128]{1,0:T(8,128)S(1)}, u32[]{:S(2)}, u32[]{:S(2)}) collective-permute-start(f32[256,128]{1,0:T(8,128)} %get-tuple-element.11), channel_id=1, source_target_pairs={{0,8},{16,24},{32,40},{48,56},{64,72},{80,88},{96,104},{112,120},{... | collective-permute-start | bytes 393224 | tf_op jit(solution)/shard_map/ppermute | solution.py:530
  11.5 11.8 %collective-permute-start = (f32[256,128]{1,0:T(8,128)}, f32[256,128]{1,0:T(8,128)S(1)}, u32[]{:S(2)}, u32[]{:S(2)}) collective-permute-start(f32[256,128]{1,0:T(8,128)} %get-tuple-element.8._sent), channel_id=1, source_target_pairs={{8,16},{24,32},{40,48},{56,64},{72,80},{88,96},{104,112},{120,128}... | collective-permute-start | bytes 393224 | tf_op jit(solution)/shard_map/ppermute | solution.py:529
  23.3 0.0 copy-start.1
  23.3 0.0 copy-start.4
  23.4 0.0 copy-start.5
  23.4 3.4 %inner_rows.1 = f32[8,64,128]{2,1,0:T(8,128)} custom-call(f32[864,128]{1,0:T(8,128)} %bitcast.6, f32[108,1,128]{2,1,0:T(1,128)} %bitcast.10, f32[108,1,128]{2,1,0:T(1,128)} %bitcast.16, f32[108,1,128]{2,1,0:T(1,128)} %bitcast.14, bf16[2,4,256,256]{3,2,1,0:T(8,128)(2,1)} %constant.6.clone.wide_far.wide_ref, ...), custom_call_target="tpu_custom_call" | custom-call | tf_op jit(solution)/shard_map/inner_rows/pallas_call | solution.py:532
  26.8 0.0 copy-start
  26.8 0.0 copy-start.2
  26.8 0.0 copy-start.6
  26.8 3.6 %all-to-all-start = ((f32[8,64,128]{2,1,0:T(8,128)}), f32[8,64,128]{2,1,0:T(8,128)S(1)}, u32[]{:S(2)}, u32[]{:S(2)}) async-start(f32[8,64,128]{2,1,0:T(8,128)} %inner_rows.1), calls=%async_computation | async-start | bytes 524288 | tf_op jit(solution)/shard_map/all_to_all | solution.py:549
  30.4 0.0 copy-done.1
  30.4 0.0 copy-done.4
  30.4 0.0 copy-done.5
  30.4 0.0 copy-done
  30.4 0.0 copy-start.3
  30.5 0.9 %outer_zonal.1 = (f32[48,1152]{1,0:T(8,128)S(1)}, f32[16,1152]{1,0:T(8,128)S(1)}) custom-call(f32[864,128]{1,0:T(8,128)S(1)} %bitcast.7, f32[108,1,128]{2,1,0:T(1,128)S(1)} %bitcast.11, f32[108,1,128]{2,1,0:T(1,128)S(1)} %bitcast.17, bf16[2,4,256,256]{3,2,1,0:T(8,128)(2,1)S(1)} %copy-done.1, bf16[2,128,128]{2,1,0:T(8,128)(2,1)S(1)} %copy-done.4, ...), custom_call_target="tpu_custom_call" | custom-call | flops 20000000000 | bytes 10000000000 | tf_op jit(solution)/shard_map/outer_zonal/pallas_call | solution.py:550
  31.4 0.0 collective-permute-done.1.even_ref
  31.4 3.3 %collective-permute-done.odd_ref = f32[256,128]{1,0:T(8,128)S(1)} collective-permute-done((f32[256,128]{1,0:T(8,128)}, f32[256,128]{1,0:T(8,128)S(1)}, u32[]{:S(2)}, u32[]{:S(2)}) %collective-permute-start) | collective-permute-done | bytes 131104 | tf_op jit(solution)/shard_map/ppermute | solution.py:529
  34.6 0.9 %outer_rows.1 = f32[8,64,128]{2,1,0:T(8,128)S(1)} custom-call(f32[864,128]{1,0:T(8,128)S(1)} %bitcast.8, f32[48,1152]{1,0:T(8,128)S(1)} %get-tuple-element.9.z_ref, f32[16,1152]{1,0:T(8,128)S(1)} %get-tuple-element.10.base_ref, f32[108,1,128]{2,1,0:T(1,128)S(1)} %bitcast.12, f32[108,1,128]{2,1,0:T(1,128)S(1)} %bitcast.15, ...), custom_call_target="tpu_custom_call" | custom-call | tf_op jit(solution)/shard_map/outer_rows/pallas_call | solution.py:562
  35.5 0.0 copy-start.7
  35.5 4.5 %all-to-all-done.first_ref = f32[8,64,128]{2,1,0:T(8,128)S(1)} async-done(((f32[8,64,128]{2,1,0:T(8,128)}), f32[8,64,128]{2,1,0:T(8,128)S(1)}, u32[]{:S(2)}, u32[]{:S(2)}) %all-to-all-start) | async-done | bytes 262176 | tf_op jit(solution)/shard_map/all_to_all | solution.py:549
  40.0 12.1 %all_to_all.10.second_ref = f32[8,64,128]{2,1,0:T(8,128)S(1)} all-to-all(f32[8,64,128]{2,1,0:T(8,128)S(1)} %outer_rows.1), channel_id=1, replica_groups=mesh['lat'=64,'lev'=8] {'lev'}, dimensions={0} | all-to-all | bytes 524288 | tf_op jit(solution)/shard_map/all_to_all | solution.py:574
  52.2 2.1 %remap.1 = (f32[8,12,8,144]{3,2,1,0:T(8,128)}, f32[12,144]{1,0:T(8,128)}) custom-call(f32[8]{0:T(128)S(1)} %copy-done.7, f32[8,64,128]{2,1,0:T(8,128)S(1)} %all-to-all-done.first_ref, f32[8,64,128]{2,1,0:T(8,128)S(1)} %all_to_all.10.second_ref), custom_call_target="tpu_custom_call" | custom-call | tf_op jit(solution)/shard_map/remap/pallas_call | solution.py:575
  (4 shorter events, 0.0 us)
Async XLA Ops:
  2.4 28.9 %collective-permute-start.1 = (f32[256,128]{1,0:T(8,128)}, f32[256,128]{1,0:T(8,128)S(1)}, u32[]{:S(2)}, u32[]{:S(2)}) collective-permute-start(f32[256,128]{1,0:T(8,128)} %get-tuple-element.11), channel_id=1, source_target_pairs={{0,8},{16,24},{32,40},{48,56},{64,72},{80,88},{96,104},{112,120},{... | collective-permute-start | bytes 393224 | tf_op jit(solution)/shard_map/ppermute | solution.py:530
  11.5 23.1 %collective-permute-start = (f32[256,128]{1,0:T(8,128)}, f32[256,128]{1,0:T(8,128)S(1)}, u32[]{:S(2)}, u32[]{:S(2)}) collective-permute-start(f32[256,128]{1,0:T(8,128)} %get-tuple-element.8._sent), channel_id=1, source_target_pairs={{8,16},{24,32},{40,48},{56,64},{72,80},{88,96},{104,112},{120,128}... | collective-permute-start | bytes 393224 | tf_op jit(solution)/shard_map/ppermute | solution.py:529
  23.3 7.0 %copy-start.1 = (bf16[2,4,256,256]{3,2,1,0:T(8,128)(2,1)S(1)}, bf16[2,4,256,256]{3,2,1,0:T(8,128)(2,1)}, u32[]{:S(2)}) copy-start(bf16[2,4,256,256]{3,2,1,0:T(8,128)(2,1)} %constant.6.clone.wide_far.wide_ref) | copy-start | bytes 3145732
  23.3 7.0 %copy-start.4 = (bf16[2,128,128]{2,1,0:T(8,128)(2,1)S(1)}, bf16[2,128,128]{2,1,0:T(8,128)(2,1)}, u32[]{:S(2)}) copy-start(bf16[2,128,128]{2,1,0:T(8,128)(2,1)} %constant.7.clone.zero_far.zero_ref) | copy-start | bytes 196612
  23.4 7.0 %copy-start.5 = (f32[1,12,1152]{2,0,1:T(1,128)S(1)}, f32[1,12,1152]{2,0,1:T(1,128)}, u32[]{:S(2)}) copy-start(f32[1,12,1152]{2,0,1:T(1,128)} %param.10) | copy-start | bytes 165892
  26.8 3.6 %copy-start = (f32[8,1,12,1152]{3,1,2,0:T(1,128)S(1)}, f32[8,1,12,1152]{3,1,2,0:T(1,128)}, u32[]{:S(2)}) copy-start(f32[8,1,12,1152]{3,1,2,0:T(1,128)} %param.8) | copy-start | bytes 1327108
  26.8 3.6 %copy-start.2 = (f32[1,12,1152]{2,0,1:T(1,128)S(1)}, f32[1,12,1152]{2,0,1:T(1,128)}, u32[]{:S(2)}) copy-start(f32[1,12,1152]{2,0,1:T(1,128)} %param.9) | copy-start | bytes 165892
  26.8 3.6 %copy-start.6 = (f32[8,640]{1,0:T(8,128)S(1)}, f32[8,640]{1,0:T(8,128)}, u32[]{:S(2)}) copy-start(f32[8,640]{1,0:T(8,128)} %constant.8.clone.table_far.table_ref) | copy-start | bytes 61444
  26.8 13.2 %all-to-all-start = ((f32[8,64,128]{2,1,0:T(8,128)}), f32[8,64,128]{2,1,0:T(8,128)S(1)}, u32[]{:S(2)}, u32[]{:S(2)}) async-start(f32[8,64,128]{2,1,0:T(8,128)} %inner_rows.1), calls=%async_computation | async-start | bytes 524288 | tf_op jit(solution)/shard_map/all_to_all | solution.py:549
  30.4 4.2 %copy-start.3 = (f32[1,12,1152]{2,0,1:T(1,128)S(1)}, f32[1,12,1152]{2,0,1:T(1,128)}, u32[]{:S(2)}) copy-start(f32[1,12,1152]{2,0,1:T(1,128)} %param.11) | copy-start | bytes 165892
  35.5 16.7 %copy-start.7 = (f32[8]{0:T(128)S(1)}, f32[8]{0:T(128)}, u32[]{:S(2)}) copy-start(f32[8]{0:T(128)} %weight_ref.1) | copy-start | bytes 100

commit v3 on v2

--- a/solution.py
+++ b/solution.py
@@ -27,6 +27,7 @@
 ZFLOPS = 2 * 10**10
 ZBYTES = 10**10
 WHOLE = 62
+RFLOPS = 10000000000
 F32 = jnp.float32
 BF16 = jnp.bfloat16
 
@@ -166,40 +167,18 @@
     return ref[pl.ds(CHUNKS * row + chunk, NT, stride=CHUNKS * ROWS), :]
 
 
-def edge_kernel(
-    q_in, h_in, cy_in,
-    odd_ref, even_ref,
-    q_ref, h_ref, cy_ref, semaphores,
-):
-    band = lax.axis_index("lat")
-    loads = copies(semaphores, (q_in, q_ref), (h_in, h_ref), (cy_in, cy_ref))
-    for load in loads:
-        load.start()
-    for load in loads:
-        load.wait()
-
-    def put(ref, first):
-        for i in range(HALO):
-            for c in range(CHUNKS):
-                at = 8 * (CHUNKS * i + c)
-                ref[at : at + 8, :] = tracer_tile(q_ref, first + i, c)
-        at = 8 * CHUNKS * HALO
-        size = CHUNKS * HALO
-        for i in range(size):
-            ref[at + i : at + i + 1, :] = h_ref[CHUNKS * first + i]
-        for i in range(CHUNKS):
-            ref[at + size + i : at + size + i + 1, :] = cy_ref[i]
-        ref[at + size + CHUNKS : SEND, :] = jnp.zeros((SEND - at - size - CHUNKS, LANES), F32)
-
-    @pl.when(band % 2 == 0)
-    def _():
-        put(even_ref, ROWS - HALO)
-        put(odd_ref, 0)
-
-    @pl.when(band % 2 == 1)
-    def _():
-        put(odd_ref, ROWS - HALO)
-        put(even_ref, 0)
+def put_edge(ref, first, q_ref, h_ref, cy_ref):
+    for i in range(HALO):
+        for c in range(CHUNKS):
+            at = 8 * (CHUNKS * i + c)
+            ref[at : at + 8, :] = tracer_tile(q_ref, first + i, c)
+    at = 8 * CHUNKS * HALO
+    size = CHUNKS * HALO
+    for i in range(size):
+        ref[at + i : at + i + 1, :] = h_ref[CHUNKS * first + i]
+    for i in range(CHUNKS):
+        ref[at + size + i : at + size + i + 1, :] = cy_ref[i]
+    ref[at + size + CHUNKS : SEND, :] = jnp.zeros((SEND - at - size - CHUNKS, LANES), F32)
 
 
 def split_bf16(x):
@@ -353,33 +332,33 @@
     return jnp.concatenate([tracer_tile(ref, row, chunk) for chunk in range(CHUNKS)], axis=1)
 
 
-def inner_kernel(
-    q_far, h_far, cx_far, cy_far, wide_far, zero_far, table_far, _sent,
-    msg,
-    cx_scr, hx_scr, cy_scr, e_scr, wx_scr, wy_scr, z_scr, spec_scr, q_scr,
-    q_in, h_in, cx_in, cy_in, wide_ref, zero_ref, table_ref, semaphores,
-):
-    band = lax.axis_index("lat")
-    *fields, wide_load, zero_load, table_load = copies(
-        semaphores, (q_far, q_in), (h_far, h_in), (cx_far, cx_in), (cy_far, cy_in),
-        (wide_far, wide_ref), (zero_far, zero_ref), (table_far, table_ref),
-    )
-    loads = (wide_load, zero_load, table_load)
+def is_early(band):
+    return band % 4 < 2
+
+
+def inner_work(band, far_refs, near_refs, msg_far, work, semaphores, loaded):
+    msg, cx_scr, hx_scr, cy_scr, e_scr, wx_scr, wy_scr, z_scr, spec_scr, q_scr = work
+    q_in, h_in, cy_in, cx_in, wide_ref, zero_ref, table_ref = near_refs
+    loads = [
+        pltpu.make_async_copy(far_refs[i], near_refs[i], semaphores.at[i]) for i in range(loaded, 7)
+    ]
+    fields, tables = loads[: 4 - loaded], loads[4 - loaded :]
     for load in fields:
         load.start()
 
     @pl.when(is_polar(band))
     def _():
-        for load in loads:
+        for load in tables:
             load.start()
 
+    for load in fields:
+        load.wait()
+
     def smooth_rows(band):
-        for load in loads:
+        for load in tables:
             load.wait()
         smooth(band, INNER, z_scr, spec_scr, wide_ref, zero_ref, table_ref)
 
-    for load in fields:
-        load.wait()
     base = zonal(INNER, q_in, h_in, cx_in, cx_scr, hx_scr, wx_scr, z_scr, smooth_rows)
     spread(cy_in, cy_scr, 0)
     cy_scr[ROWS:16] = jnp.zeros((4, NLON), F32)
@@ -392,6 +371,45 @@
         return combine(r, wy_scr, lambda j: q_scr[j], z_scr[NT * v : NT * (v + 1), :])
 
     pack_message(INNER, ratio_row, new_thick, msg)
+    move = pltpu.make_async_copy(msg, msg_far, semaphores.at[7])
+    move.start()
+    move.wait()
+
+
+def edge_kernel(*refs):
+    far_refs, (odd_ref, even_ref, msg_far), near_refs = refs[:7], refs[7:10], refs[10:17]
+    work, semaphores = refs[17:27], refs[27]
+    q_ref, h_ref, cy_ref = near_refs[:3]
+    band = lax.axis_index("lat")
+    loads = copies(semaphores, *zip(far_refs[:3], near_refs[:3]))
+    for load in loads:
+        load.start()
+    for load in loads:
+        load.wait()
+
+    @pl.when(band % 2 == 0)
+    def _():
+        put_edge(even_ref, ROWS - HALO, q_ref, h_ref, cy_ref)
+        put_edge(odd_ref, 0, q_ref, h_ref, cy_ref)
+
+    @pl.when(band % 2 == 1)
+    def _():
+        put_edge(odd_ref, ROWS - HALO, q_ref, h_ref, cy_ref)
+        put_edge(even_ref, 0, q_ref, h_ref, cy_ref)
+
+    @pl.when(is_early(band))
+    def _():
+        inner_work(band, far_refs, near_refs, msg_far, work, semaphores, 3)
+
+
+def inner_kernel(*refs):
+    far_refs, msg_far, near_refs = refs[:7], refs[10], refs[11:18]
+    work, semaphores = refs[18:28], refs[28]
+    band = lax.axis_index("lat")
+
+    @pl.when(jnp.logical_not(is_early(band)))
+    def _():
+        inner_work(band, far_refs, near_refs, msg_far, work, semaphores, 0)
 
 
 def zonal_kernel(
@@ -451,46 +469,56 @@
     pack_message(OUTER, ratio_row, new_thick, msg)
 
 
-def remap_kernel(weight_ref, first_ref, second_ref, out_ref, mass_ref, inter_scr):
+def remap_half(rows, places, weight_ref, in_ref, out_ref, mass_ref, inter_scr):
     weight_sum = weight_ref[0]
     for k in range(1, NLEV):
         weight_sum = weight_sum + weight_ref[k]
     base = 8 * HALF + 8
-    for in_ref, rows in ((first_ref, INNER), (second_ref, OUTER)):
-        thick = [in_ref[i, base : base + 8, :] for i in range(NLEV)]
-        upper, lower = [thick[0]], []
-        for i in range(1, NLEV):
-            upper.append(upper[-1] + thick[i])
+    thick = [in_ref[i, base : base + 8, :] for i in range(NLEV)]
+    upper, lower = [thick[0]], []
+    for i in range(1, NLEV):
+        upper.append(upper[-1] + thick[i])
+    for i in range(NLEV):
+        lower.append(upper[i] - thick[i])
+    total = upper[-1]
+    for v, r in enumerate(rows):
+        mass_ref[r : r + 1, 0:LANES] = total[v : v + 1]
+        mass_ref[r : r + 1, LANES:PIECE] = turn(total[HALF : HALF + 1], -TAIL * v)[:, :TAIL]
+    reach = None
+    for k in range(NLEV):
+        target = total * (weight_ref[k] / weight_sum)
+        reach = target if reach is None else reach + target
+        start = reach - target
+        scale = 1.0 / target
         for i in range(NLEV):
-            lower.append(upper[i] - thick[i])
-        total = upper[-1]
-        for v, r in enumerate(rows):
-            mass_ref[r : r + 1, 0:LANES] = total[v : v + 1]
-            mass_ref[r : r + 1, LANES:PIECE] = turn(total[HALF : HALF + 1], -TAIL * v)[:, :TAIL]
-        reach = None
-        for k in range(NLEV):
-            target = total * (weight_ref[k] / weight_sum)
-            reach = target if reach is None else reach + target
-            start = reach - target
-            scale = 1.0 / target
-            for i in range(NLEV):
-                overlap = jnp.minimum(upper[i], reach) - jnp.maximum(lower[i], start)
-                at = 8 * (NLEV * i + k)
-                inter_scr[at : at + 8, :] = jnp.maximum(overlap, 0.0) * scale
-        for v in range(HALF + 1):
-            moved = [None] * NT
-            for i in range(NLEV):
-                share = inter_scr[pl.ds(8 * NLEV * i + v, NLEV, stride=8), :]
-                for t in range(NT):
-                    at = 8 * v + t
-                    term = jnp.broadcast_to(in_ref[i, at : at + 1, :], (NLEV, LANES)) * share
-                    moved[t] = term if i == 0 else moved[t] + term
+            overlap = jnp.minimum(upper[i], reach) - jnp.maximum(lower[i], start)
+            at = 8 * (NLEV * i + k)
+            inter_scr[at : at + 8, :] = jnp.maximum(overlap, 0.0) * scale
+    for v in range(HALF + 1):
+        moved = [None] * NT
+        for i in range(NLEV):
+            share = inter_scr[pl.ds(8 * NLEV * i + v, NLEV, stride=8), :]
             for t in range(NT):
-                if v < HALF:
-                    out_ref[t, rows[v], :, 0:LANES] = moved[t]
-                else:
-                    for u, r in enumerate(rows):
-                        out_ref[t, r, :, LANES:PIECE] = turn(moved[t], -TAIL * u)[:, :TAIL]
+                at = 8 * v + t
+                term = jnp.broadcast_to(in_ref[i, at : at + 1, :], (NLEV, LANES)) * share
+                moved[t] = term if i == 0 else moved[t] + term
+        for t in range(NT):
+            if v < HALF:
+                out_ref[t, places[v], :, 0:LANES] = moved[t]
+            else:
+                for u in range(HALF):
+                    out_ref[t, places[u], :, LANES:PIECE] = turn(moved[t], -TAIL * u)[:, :TAIL]
+
+
+def inner_remap_kernel(weight_ref, in_ref, out_ref, mass_ref, inter_scr):
+    mass_ref[...] = jnp.zeros(mass_ref.shape, F32)
+    remap_half(INNER, range(HALF), weight_ref, in_ref, out_ref, mass_ref, inter_scr)
+
+
+def outer_remap_kernel(weight_ref, in_ref, inner_ref, inner_mass, out_ref, mass_ref, inter_scr):
+    mass_ref[...] = inner_mass[...]
+    out_ref[:, HALO : ROWS - HALO] = inner_ref[...]
+    remap_half(OUTER, OUTER, weight_ref, in_ref, out_ref, mass_ref, inter_scr)
 
 
 def swaps(first, bands):
@@ -513,39 +541,43 @@
     h_in, cx_in, cy_in = (
         field.reshape(ROWS * CHUNKS, 1, LANES) for field in (thickness, courant_x, courant_y)
     )
-    odd, even = pl.pallas_call(
-        edge_kernel,
-        out_shape=(shape(SEND, LANES),) * 2,
-        in_specs=[far()] * 3,
-        out_specs=(vmem(),) * 2,
-        scratch_shapes=[
-            scratch(NT * ROWS * CHUNKS, LANES), scratch(ROWS * CHUNKS, 1, LANES),
-            scratch(ROWS * CHUNKS, 1, LANES), pltpu.SemaphoreType.DMA((3,)),
-        ],
-        compiler_params=params(WHOLE),
-        name="edge_rows",
-    )(q_in, h_in, cy_in)
-    sent = odd
-    odd = lax.ppermute(odd, "lat", swaps(1, bands))
-    even = lax.ppermute(even, "lat", swaps(0, bands))
-    tables = (jnp.asarray(wide), jnp.asarray(zero), jnp.asarray(table))
-    first = pl.pallas_call(
-        inner_kernel,
-        out_shape=shape(NLEV, MSG, LANES),
-        in_specs=[far()] * 8,
-        out_specs=vmem(),
-        scratch_shapes=[
+    tables = tuple(jnp.asarray(t) for t in (wide, zero, table))
+    operands = (q_in, h_in, cy_in, cx_in, *tables)
+    room = (
+        [scratch(NT * ROWS * CHUNKS, LANES)]
+        + [scratch(ROWS * CHUNKS, 1, LANES)] * 3
+        + [pltpu.VMEM(t.shape, t.dtype) for t in tables]
+        + [
+            scratch(NLEV, MSG, LANES),
             scratch(16, NLON), scratch(24, NLON), scratch(16, NLON), scratch(24, NLON),
             scratch(7, 16, NLON), scratch(8, 16, NLON),
             scratch(HALF * NT, NLON), scratch(HALF * NT, NLON), scratch(ROWS, NT, NLON),
-            scratch(NT * ROWS * CHUNKS, LANES),
+            pltpu.SemaphoreType.DMA((8,)),
         ]
-        + [scratch(ROWS * CHUNKS, 1, LANES)] * 3
-        + [pltpu.VMEM(t.shape, t.dtype) for t in tables]
-        + [pltpu.SemaphoreType.DMA((7,))],
+    )
+    odd, even, message = pl.pallas_call(
+        edge_kernel,
+        out_shape=(shape(SEND, LANES),) * 2 + (shape(NLEV, MSG, LANES),),
+        in_specs=[far()] * 7,
+        out_specs=(vmem(),) * 2 + (far(),),
+        scratch_shapes=room,
+        compiler_params=params(WHOLE),
+        name="edge_rows",
+    )(*operands)
+    sent = (odd, even)
+    odd = lax.ppermute(odd, "lat", swaps(1, bands))
+    even = lax.ppermute(even, "lat", swaps(0, bands))
+    message = pl.pallas_call(
+        inner_kernel,
+        out_shape=shape(NLEV, MSG, LANES),
+        in_specs=[far()] * 10,
+        out_specs=far(),
+        scratch_shapes=room,
+        input_output_aliases={7: 0},
         compiler_params=params(WHOLE),
         name="inner_rows",
-    )(q_in, h_in, cx_in, cy_in, *tables, sent)
+    )(*operands, message, *sent)
+    first = message
     first = lax.all_to_all(first, "lev", split_axis=0, concat_axis=0, tiled=True)
     z, base = pl.pallas_call(
         zonal_kernel,
@@ -572,15 +604,26 @@
         name="outer_rows",
     )(q_in, z, base, h_in, cy_in, odd, even)
     second = lax.all_to_all(second, "lev", split_axis=0, concat_axis=0, tiled=True)
-    remapped, column_mass = pl.pallas_call(
-        remap_kernel,
-        out_shape=(shape(NT, ROWS, NLEV, PIECE), shape(ROWS, PIECE)),
-        in_specs=[pl.BlockSpec(memory_space=pltpu.SMEM), vmem(), vmem()],
+    smem = pl.BlockSpec(memory_space=pltpu.SMEM)
+    inner_out, inner_mass = pl.pallas_call(
+        inner_remap_kernel,
+        out_shape=(shape(NT, HALF, NLEV, PIECE), shape(ROWS, PIECE)),
+        in_specs=[smem, vmem()],
         out_specs=(vmem(),) * 2,
         scratch_shapes=[scratch(NLEV * NLEV * 8, LANES)],
         compiler_params=params(32),
-        name="remap",
-    )(level_weights, first, second)
+        cost_estimate=pl.CostEstimate(flops=RFLOPS, bytes_accessed=RFLOPS, transcendentals=0),
+        name="inner_remap",
+    )(level_weights, first)
+    remapped, column_mass = pl.pallas_call(
+        outer_remap_kernel,
+        out_shape=(shape(NT, ROWS, NLEV, PIECE), shape(ROWS, PIECE)),
+        in_specs=[smem] + [vmem()] * 3,
+        out_specs=(vmem(),) * 2,
+        scratch_shapes=[scratch(NLEV * NLEV * 8, LANES)],
+        compiler_params=params(32),
+        name="outer_remap",
+    )(level_weights, second, inner_out, inner_mass)
     return jnp.transpose(remapped, (0, 2, 1, 3)), column_mass
 
 

time: 54.6 us -> 54.7 us (level)
  waiting for transfers between devices: 7.78 us -> 19.9 us
  blocking collectives: 12.1 us -> 0 us
  starting transfers between devices: 24.5 us -> 23.1 us
  Pallas kernels: 9.08 us -> 10 us
    all_to_all x1 -> x0, blocking collectives: 12.1 us -> none  [local(): lax.all_to_all(second, 'lev', split_axis=0, concat_axis=0, tiled=True)]
    all_to_all x0 -> x1, waiting for transfers between devices: none -> 8.87 us  [local(): lax.all_to_all(second, 'lev', split_axis=0, concat_axis=0, tiled=True)]
    ppermute x1, waiting for transfers between devices: 0.01 us -> 7.4 us  [local(): even = lax.ppermute(even, 'lat', swaps(0, bands))]
    ppermute x1, starting transfers between devices: 9.1 us -> 2.75 us  [local(): even = lax.ppermute(even, 'lat', swaps(0, bands))]
    all_to_all x1, waiting for transfers between devices: 4.52 us -> 0.01 us  [local(): lax.all_to_all(first, 'lev', split_axis=0, concat_axis=0, tiled=True)]
    all_to_all x0 -> x1, starting transfers between devices: none -> 4.42 us  [local(): lax.all_to_all(second, 'lev', split_axis=0, concat_axis=0, tiled=True)]
    pallas_call x2 -> x3, Pallas kernels: 3.91 us -> 7.46 us  [the longest x1 4.85 us: local(): pl.pallas_call(edge_kernel, out_shape=(shape(SEND, LANES),) * 2 + (shape(...]
    pallas_call x1, Pallas kernels: 3.4 us -> 0.09 us  [local(): pl.pallas_call(inner_kernel, out_shape=shape(NLEV, MSG, LANES), in_specs=...]
  transfers between devices with their start and end apart: 3 -> 4, of which waited for: 2 -> 3; matrix products, arithmetic and copies ran while one was open for 0% -> 0% of each run, Pallas kernels for 10% -> 6%
where the time goes in v3:
time: 54.7 us; the launch traced here: 54 us
  starting transfers between devices  23.1 us (42%)
  waiting for transfers between devices  19.9 us (36%)
  Pallas kernels  10 us (18%)
  between operations  0.79 us (1%)
    ppermute x1, starting transfers between devices, local(): odd = lax.ppermute(odd, 'lat', swaps(1, bands))  12.4 us
    all_to_all x1, waiting for transfers between devices, local(): lax.all_to_all(second, 'lev', split_axis=0, concat_axis=0, tiled=True)  8.87 us
    ppermute x1, waiting for transfers between devices, local(): even = lax.ppermute(even, 'lat', swaps(0, bands))  7.4 us
    pallas_call x1, Pallas kernels, local(): pl.pallas_call(edge_kernel, out_shape=(shape(SEND, LANES),) * 2 + (shape(...  4.85 us
    all_to_all x1, starting transfers between devices, local(): lax.all_to_all(second, 'lev', split_axis=0, concat_axis=0, tiled=True)  4.42 us
    ppermute x1, waiting for transfers between devices, local(): odd = lax.ppermute(odd, 'lat', swaps(1, bands))  3.67 us
    all_to_all x1, starting transfers between devices, local(): lax.all_to_all(first, 'lev', split_axis=0, concat_axis=0, tiled=True)  3.56 us
    ppermute x1, starting transfers between devices, local(): even = lax.ppermute(even, 'lat', swaps(0, bands))  2.75 us
  transfers between devices with their start and end apart: 4, of which 3 were waited for; matrix products, arithmetic and copies ran while one was open for 0% of the time, Pallas kernels for 6%

profile of v3, /device:TPU:6, one launch (start us, length us, event | category | flops | bytes accessed | tf_op | source)
XLA Modules:
  0.0 54.0 jit_solution(419712085825484122)
XLA Ops:
  0.6 4.9 %edge_rows.1 = (f32[256,128]{1,0:T(8,128)}, f32[256,128]{1,0:T(8,128)}, f32[8,64,128]{2,1,0:T(8,128)}) custom-call(f32[864,128]{1,0:T(8,128)} %bitcast.5, f32[108,1,128]{2,1,0:T(1,128)} %bitcast.9, f32[108,1,128]{2,1,0:T(1,128)} %bitcast.13, f32[108,1,128]{2,1,0:T(1,128)} %bitcast.16, bf16[2,4,256,256]{3,2,1,0:T(8,128)(2,1)} %constant.6.clone.wide_ref.refs_4_, ...), custom_call_target="tpu_custom_call" | custom-call | tf_op jit(solution)/shard_map/edge_rows/pallas_call | solution.py:558
  5.5 12.4 %collective-permute-start = (f32[256,128]{1,0:T(8,128)}, f32[256,128]{1,0:T(8,128)S(1)}, u32[]{:S(2)}, u32[]{:S(2)}) collective-permute-start(f32[256,128]{1,0:T(8,128)} %get-tuple-element.13.refs_8_), channel_id=1, source_target_pairs={{8,16},{24,32},{40,48},{56,64},{72,80},{88,96},{104,112},{120,128}... | collective-permute-start | bytes 393224 | tf_op jit(solution)/shard_map/ppermute | solution.py:568
  17.9 2.7 %collective-permute-start.1 = (f32[256,128]{1,0:T(8,128)}, f32[256,128]{1,0:T(8,128)S(1)}, u32[]{:S(2)}, u32[]{:S(2)}) collective-permute-start(f32[256,128]{1,0:T(8,128)} %get-tuple-element.14.refs_9_), channel_id=1, source_target_pairs={{0,8},{16,24},{32,40},{48,56},{64,72},{80,88},{96,104},{112,120},{... | collective-permute-start | bytes 393224 | tf_op jit(solution)/shard_map/ppermute | solution.py:569
  20.7 0.0 copy-start
  20.7 0.0 copy-start.4
  20.7 0.0 copy-start.5
  20.7 0.1 inner_rows.1
  20.8 0.0 copy-start.1
  20.8 0.0 copy-start.2
  20.8 0.0 copy-start.6
  20.8 3.6 %all-to-all-start.1 = ((f32[8,64,128]{2,1,0:T(8,128)}), f32[8,64,128]{2,1,0:T(8,128)S(1)}, u32[]{:S(2)}, u32[]{:S(2)}) async-start(f32[8,64,128]{2,1,0:T(8,128)} %inner_rows.1), calls=%async_computation.1 | async-start | bytes 524288 | tf_op jit(solution)/shard_map/all_to_all | solution.py:581
  24.4 0.0 copy-done
  24.4 0.0 copy-done.4
  24.4 0.0 copy-done.5
  24.5 0.0 copy-start.3
  24.5 0.9 %outer_zonal.1 = (f32[48,1152]{1,0:T(8,128)S(1)}, f32[16,1152]{1,0:T(8,128)S(1)}) custom-call(f32[864,128]{1,0:T(8,128)S(1)} %bitcast.7, f32[108,1,128]{2,1,0:T(1,128)S(1)} %bitcast.11, f32[108,1,128]{2,1,0:T(1,128)S(1)} %bitcast.18, bf16[2,4,256,256]{3,2,1,0:T(8,128)(2,1)S(1)} %copy-done, bf16[2,128,128]{2,1,0:T(8,128)(2,1)S(1)} %copy-done.4, ...), custom_call_target="tpu_custom_call" | custom-call | flops 20000000000 | bytes 10000000000 | tf_op jit(solution)/shard_map/outer_zonal/pallas_call | solution.py:582
  25.4 3.7 %collective-permute-done.odd_ref = f32[256,128]{1,0:T(8,128)S(1)} collective-permute-done((f32[256,128]{1,0:T(8,128)}, f32[256,128]{1,0:T(8,128)S(1)}, u32[]{:S(2)}, u32[]{:S(2)}) %collective-permute-start) | collective-permute-done | bytes 131104 | tf_op jit(solution)/shard_map/ppermute | solution.py:568
  29.0 7.4 %collective-permute-done.1.even_ref = f32[256,128]{1,0:T(8,128)S(1)} collective-permute-done((f32[256,128]{1,0:T(8,128)}, f32[256,128]{1,0:T(8,128)S(1)}, u32[]{:S(2)}, u32[]{:S(2)}) %collective-permute-start.1) | collective-permute-done | bytes 131104 | tf_op jit(solution)/shard_map/ppermute | solution.py:569
  36.4 1.6 %outer_rows.1 = f32[8,64,128]{2,1,0:T(8,128)} custom-call(f32[864,128]{1,0:T(8,128)S(1)} %bitcast.8, f32[48,1152]{1,0:T(8,128)S(1)} %get-tuple-element.11.z_ref, f32[16,1152]{1,0:T(8,128)S(1)} %get-tuple-element.12.base_ref, f32[108,1,128]{2,1,0:T(1,128)S(1)} %bitcast.12, f32[108,1,128]{2,1,0:T(1,128)S(1)} %bitcast.15, ...), custom_call_target="tpu_custom_call" | custom-call | tf_op jit(solution)/shard_map/outer_rows/pallas_call | solution.py:594
  38.0 0.0 all-to-all-done.1.in_ref
  38.0 4.4 %all-to-all-start = ((f32[8,64,128]{2,1,0:T(8,128)}), f32[8,64,128]{2,1,0:T(8,128)S(1)}, u32[]{:S(2)}, u32[]{:S(2)}) async-start(f32[8,64,128]{2,1,0:T(8,128)} %outer_rows.1), calls=%async_computation | async-start | bytes 524288 | tf_op jit(solution)/shard_map/all_to_all | solution.py:606
  42.5 0.9 %inner_remap.1 = (f32[8,6,8,144]{3,2,1,0:T(8,128)S(1)}, f32[12,144]{1,0:T(8,128)S(1)}) custom-call(f32[8]{0:T(128)S(1)} %copy-done.7, f32[8,64,128]{2,1,0:T(8,128)S(1)} %all-to-all-done.1.in_ref), custom_call_target="tpu_custom_call" | custom-call | flops 10000000000 | bytes 10000000000 | tf_op jit(solution)/shard_map/inner_remap/pallas_call | solution.py:608
  43.3 8.9 %all-to-all-done.in_ref = f32[8,64,128]{2,1,0:T(8,128)S(1)} async-done(((f32[8,64,128]{2,1,0:T(8,128)}), f32[8,64,128]{2,1,0:T(8,128)S(1)}, u32[]{:S(2)}, u32[]{:S(2)}) %all-to-all-start) | async-done | bytes 262176 | tf_op jit(solution)/shard_map/all_to_all | solution.py:606
  52.2 1.8 %outer_remap.1 = (f32[8,12,8,144]{3,2,1,0:T(8,128)}, f32[12,144]{1,0:T(8,128)}) custom-call(f32[8]{0:T(128)S(1)} %copy-done.7, f32[8,64,128]{2,1,0:T(8,128)S(1)} %all-to-all-done.in_ref, f32[8,6,8,144]{3,2,1,0:T(8,128)S(1)} %get-tuple-element.16.inner_ref, f32[12,144]{1,0:T(8,128)S(1)} %get-tuple-element.17.inner_mass), custom_call_target="tpu_custom_call" | custom-call | tf_op jit(solution)/shard_map/outer_remap/pallas_call | solution.py:618
  (6 shorter events, 0.0 us)
Async XLA Ops:
  5.5 23.5 %collective-permute-start = (f32[256,128]{1,0:T(8,128)}, f32[256,128]{1,0:T(8,128)S(1)}, u32[]{:S(2)}, u32[]{:S(2)}) collective-permute-start(f32[256,128]{1,0:T(8,128)} %get-tuple-element.13.refs_8_), channel_id=1, source_target_pairs={{8,16},{24,32},{40,48},{56,64},{72,80},{88,96},{104,112},{120,128}... | collective-permute-start | bytes 393224 | tf_op jit(solution)/shard_map/ppermute | solution.py:568
  17.9 18.5 %collective-permute-start.1 = (f32[256,128]{1,0:T(8,128)}, f32[256,128]{1,0:T(8,128)S(1)}, u32[]{:S(2)}, u32[]{:S(2)}) collective-permute-start(f32[256,128]{1,0:T(8,128)} %get-tuple-element.14.refs_9_), channel_id=1, source_target_pairs={{0,8},{16,24},{32,40},{48,56},{64,72},{80,88},{96,104},{112,120},{... | collective-permute-start | bytes 393224 | tf_op jit(solution)/shard_map/ppermute | solution.py:569
  20.7 3.7 %copy-start = (bf16[2,4,256,256]{3,2,1,0:T(8,128)(2,1)S(1)}, bf16[2,4,256,256]{3,2,1,0:T(8,128)(2,1)}, u32[]{:S(2)}) copy-start(bf16[2,4,256,256]{3,2,1,0:T(8,128)(2,1)} %constant.6.clone.wide_ref.refs_4_) | copy-start | bytes 3145732
  20.7 3.7 %copy-start.4 = (bf16[2,128,128]{2,1,0:T(8,128)(2,1)S(1)}, bf16[2,128,128]{2,1,0:T(8,128)(2,1)}, u32[]{:S(2)}) copy-start(bf16[2,128,128]{2,1,0:T(8,128)(2,1)} %constant.7.clone.zero_ref.refs_5_) | copy-start | bytes 196612
  20.7 3.7 %copy-start.5 = (f32[1,12,1152]{2,0,1:T(1,128)S(1)}, f32[1,12,1152]{2,0,1:T(1,128)}, u32[]{:S(2)}) copy-start(f32[1,12,1152]{2,0,1:T(1,128)} %param.10) | copy-start | bytes 165892
  20.8 3.6 %copy-start.1 = (f32[8,1,12,1152]{3,1,2,0:T(1,128)S(1)}, f32[8,1,12,1152]{3,1,2,0:T(1,128)}, u32[]{:S(2)}) copy-start(f32[8,1,12,1152]{3,1,2,0:T(1,128)} %param.8) | copy-start | bytes 1327108
  20.8 3.6 %copy-start.2 = (f32[1,12,1152]{2,0,1:T(1,128)S(1)}, f32[1,12,1152]{2,0,1:T(1,128)}, u32[]{:S(2)}) copy-start(f32[1,12,1152]{2,0,1:T(1,128)} %param.9) | copy-start | bytes 165892
  20.8 3.6 %copy-start.6 = (f32[8,640]{1,0:T(8,128)S(1)}, f32[8,640]{1,0:T(8,128)}, u32[]{:S(2)}) copy-start(f32[8,640]{1,0:T(8,128)} %constant.8.clone.table_ref.refs_6_) | copy-start | bytes 61444
  20.8 17.2 %all-to-all-start.1 = ((f32[8,64,128]{2,1,0:T(8,128)}), f32[8,64,128]{2,1,0:T(8,128)S(1)}, u32[]{:S(2)}, u32[]{:S(2)}) async-start(f32[8,64,128]{2,1,0:T(8,128)} %inner_rows.1), calls=%async_computation.1 | async-start | bytes 524288 | tf_op jit(solution)/shard_map/all_to_all | solution.py:581
  24.5 12.0 %copy-start.3 = (f32[1,12,1152]{2,0,1:T(1,128)S(1)}, f32[1,12,1152]{2,0,1:T(1,128)}, u32[]{:S(2)}) copy-start(f32[1,12,1152]{2,0,1:T(1,128)} %param.11) | copy-start | bytes 165892
  38.0 4.4 %copy-start.7 = (f32[8]{0:T(128)S(1)}, f32[8]{0:T(128)}, u32[]{:S(2)}) copy-start(f32[8]{0:T(128)} %weight_ref.3) | copy-start | bytes 100
  38.0 14.2 %all-to-all-start = ((f32[8,64,128]{2,1,0:T(8,128)}), f32[8,64,128]{2,1,0:T(8,128)S(1)}, u32[]{:S(2)}, u32[]{:S(2)}) async-start(f32[8,64,128]{2,1,0:T(8,128)} %outer_rows.1), calls=%async_computation | async-start | bytes 524288 | tf_op jit(solution)/shard_map/all_to_all | solution.py:606

commit v4 on v2

--- a/solution.py
+++ b/solution.py
@@ -168,8 +168,8 @@
 
 def edge_kernel(
     q_in, h_in, cy_in,
-    odd_ref, even_ref,
-    q_ref, h_ref, cy_ref, semaphores,
+    odd_far, even_far,
+    q_ref, h_ref, cy_ref, odd_ref, even_ref, semaphores, out_semaphores,
 ):
     band = lax.axis_index("lat")
     loads = copies(semaphores, (q_in, q_ref), (h_in, h_ref), (cy_in, cy_ref))
@@ -191,15 +191,19 @@
             ref[at + size + i : at + size + i + 1, :] = cy_ref[i]
         ref[at + size + CHUNKS : SEND, :] = jnp.zeros((SEND - at - size - CHUNKS, LANES), F32)
 
-    @pl.when(band % 2 == 0)
-    def _():
-        put(even_ref, ROWS - HALO)
-        put(odd_ref, 0)
-
-    @pl.when(band % 2 == 1)
-    def _():
-        put(odd_ref, ROWS - HALO)
-        put(even_ref, 0)
+    stores = copies(out_semaphores, (odd_ref, odd_far), (even_ref, even_far))
+    for parity, ref, store in ((0, odd_ref, stores[0]), (1, even_ref, stores[1])):
+        @pl.when(band % 2 == parity)
+        def _(ref=ref):
+            put(ref, 0)
+
+        @pl.when(band % 2 != parity)
+        def _(ref=ref):
+            put(ref, ROWS - HALO)
+
+        store.start()
+    for store in stores:
+        store.wait()
 
 
 def split_bf16(x):
@@ -354,7 +358,7 @@
 
 
 def inner_kernel(
-    q_far, h_far, cx_far, cy_far, wide_far, zero_far, table_far, _sent,
+    q_far, h_far, cx_far, cy_far, wide_far, zero_far, table_far, _odd, _even,
     msg,
     cx_scr, hx_scr, cy_scr, e_scr, wx_scr, wy_scr, z_scr, spec_scr, q_scr,
     q_in, h_in, cx_in, cy_in, wide_ref, zero_ref, table_ref, semaphores,
@@ -517,22 +521,23 @@
         edge_kernel,
         out_shape=(shape(SEND, LANES),) * 2,
         in_specs=[far()] * 3,
-        out_specs=(vmem(),) * 2,
+        out_specs=(far(),) * 2,
         scratch_shapes=[
             scratch(NT * ROWS * CHUNKS, LANES), scratch(ROWS * CHUNKS, 1, LANES),
-            scratch(ROWS * CHUNKS, 1, LANES), pltpu.SemaphoreType.DMA((3,)),
+            scratch(ROWS * CHUNKS, 1, LANES), scratch(SEND, LANES), scratch(SEND, LANES),
+            pltpu.SemaphoreType.DMA((3,)), pltpu.SemaphoreType.DMA((2,)),
         ],
         compiler_params=params(WHOLE),
         name="edge_rows",
     )(q_in, h_in, cy_in)
-    sent = odd
+    sent = (odd, even)
     odd = lax.ppermute(odd, "lat", swaps(1, bands))
     even = lax.ppermute(even, "lat", swaps(0, bands))
     tables = (jnp.asarray(wide), jnp.asarray(zero), jnp.asarray(table))
     first = pl.pallas_call(
         inner_kernel,
         out_shape=shape(NLEV, MSG, LANES),
-        in_specs=[far()] * 8,
+        in_specs=[far()] * 9,
         out_specs=vmem(),
         scratch_shapes=[
             scratch(16, NLON), scratch(24, NLON), scratch(16, NLON), scratch(24, NLON),
@@ -545,7 +550,7 @@
         + [pltpu.SemaphoreType.DMA((7,))],
         compiler_params=params(WHOLE),
         name="inner_rows",
-    )(q_in, h_in, cx_in, cy_in, *tables, sent)
+    )(q_in, h_in, cx_in, cy_in, *tables, *sent)
     first = lax.all_to_all(first, "lev", split_axis=0, concat_axis=0, tiled=True)
     z, base = pl.pallas_call(
         zonal_kernel,

time: 54.6 us -> 54.7 us (level)
  starting transfers between devices: 24.5 us -> 21.8 us
  waiting for transfers between devices: 7.78 us -> 10.4 us
    ppermute x1, waiting for transfers between devices: 0.01 us -> 7.11 us  [local(): even = lax.ppermute(even, 'lat', swaps(0, bands))]
    ppermute x1, starting transfers between devices: 9.1 us -> 2.74 us  [local(): even = lax.ppermute(even, 'lat', swaps(0, bands))]
    ppermute x1, starting transfers between devices: 11.8 us -> 15.4 us  [local(): odd = lax.ppermute(odd, 'lat', swaps(1, bands))]
    ppermute x1, waiting for transfers between devices: 3.26 us -> 0.71 us  [local(): odd = lax.ppermute(odd, 'lat', swaps(1, bands))]
    all_to_all x1, waiting for transfers between devices: 4.52 us -> 2.53 us  [local(): lax.all_to_all(first, 'lev', split_axis=0, concat_axis=0, tiled=True)]
  transfers between devices with their start and end apart: 3 -> 3, of which waited for: 2 -> 3; matrix products, arithmetic and copies ran while one was open for 0% -> 0% of each run, Pallas kernels for 10% -> 10%
where the time goes in v4:
time: 54.7 us; the launch traced here: 54.3 us
  starting transfers between devices  21.8 us (40%)
  blocking collectives  12.3 us (22%)
  waiting for transfers between devices  10.4 us (19%)
  Pallas kernels  9.08 us (17%)
  between operations  0.8 us (1%)
    ppermute x1, starting transfers between devices, local(): odd = lax.ppermute(odd, 'lat', swaps(1, bands))  15.4 us
    all_to_all x1, blocking collectives, local(): lax.all_to_all(second, 'lev', split_axis=0, concat_axis=0, tiled=True)  12.3 us
    ppermute x1, waiting for transfers between devices, local(): even = lax.ppermute(even, 'lat', swaps(0, bands))  7.11 us
    all_to_all x1, starting transfers between devices, local(): lax.all_to_all(first, 'lev', split_axis=0, concat_axis=0, tiled=True)  3.56 us
    pallas_call x1, Pallas kernels, local(): pl.pallas_call(inner_kernel, out_shape=shape(NLEV, MSG, LANES), in_specs=...  3.4 us
    ppermute x1, starting transfers between devices, local(): even = lax.ppermute(even, 'lat', swaps(0, bands))  2.74 us
    all_to_all x1, waiting for transfers between devices, local(): lax.all_to_all(first, 'lev', split_axis=0, concat_axis=0, tiled=True)  2.53 us
    pallas_call x1, Pallas kernels, local(): pl.pallas_call(remap_kernel, out_shape=(shape(NT, ROWS, NLEV, PIECE), sha...  2.13 us
  transfers between devices with their start and end apart: 3, of which 3 were waited for; matrix products, arithmetic and copies ran while one was open for 0% of the time, Pallas kernels for 10%

profile of v4, /device:TPU:6, one launch (start us, length us, event | category | flops | bytes accessed | tf_op | source)
XLA Modules:
  0.0 54.3 jit_solution(12566672099003631214)
XLA Ops:
  0.6 1.8 %edge_rows.1 = (f32[256,128]{1,0:T(8,128)}, f32[256,128]{1,0:T(8,128)}) custom-call(f32[864,128]{1,0:T(8,128)} %bitcast.5, f32[108,1,128]{2,1,0:T(1,128)} %bitcast.9, f32[108,1,128]{2,1,0:T(1,128)} %bitcast.13), custom_call_target="tpu_custom_call" | custom-call | tf_op jit(solution)/shard_map/edge_rows/pallas_call | solution.py:520
  2.4 15.4 %collective-permute-start = (f32[256,128]{1,0:T(8,128)}, f32[256,128]{1,0:T(8,128)S(1)}, u32[]{:S(2)}, u32[]{:S(2)}) collective-permute-start(f32[256,128]{1,0:T(8,128)} %get-tuple-element.8._odd), channel_id=1, source_target_pairs={{8,16},{24,32},{40,48},{56,64},{72,80},{88,96},{104,112},{120,128}... | collective-permute-start | bytes 393224 | tf_op jit(solution)/shard_map/ppermute | solution.py:534
  17.9 2.7 %collective-permute-start.1 = (f32[256,128]{1,0:T(8,128)}, f32[256,128]{1,0:T(8,128)S(1)}, u32[]{:S(2)}, u32[]{:S(2)}) collective-permute-start(f32[256,128]{1,0:T(8,128)} %get-tuple-element.9._even), channel_id=1, source_target_pairs={{0,8},{16,24},{32,40},{48,56},{64,72},{80,88},{96,104},{112,120},{... | collective-permute-start | bytes 393224 | tf_op jit(solution)/shard_map/ppermute | solution.py:535
  20.6 0.0 copy-start.1
  20.6 0.0 copy-start.4
  20.6 0.0 copy-start.5
  20.7 3.4 %inner_rows.1 = f32[8,64,128]{2,1,0:T(8,128)} custom-call(f32[864,128]{1,0:T(8,128)} %bitcast.6, f32[108,1,128]{2,1,0:T(1,128)} %bitcast.10, f32[108,1,128]{2,1,0:T(1,128)} %bitcast.16, f32[108,1,128]{2,1,0:T(1,128)} %bitcast.14, bf16[2,4,256,256]{3,2,1,0:T(8,128)(2,1)} %constant.6.clone.wide_far.wide_ref, ...), custom_call_target="tpu_custom_call" | custom-call | tf_op jit(solution)/shard_map/inner_rows/pallas_call | solution.py:537
  24.1 0.0 copy-start
  24.1 0.0 copy-start.2
  24.1 0.0 copy-start.6
  24.1 3.6 %all-to-all-start = ((f32[8,64,128]{2,1,0:T(8,128)}), f32[8,64,128]{2,1,0:T(8,128)S(1)}, u32[]{:S(2)}, u32[]{:S(2)}) async-start(f32[8,64,128]{2,1,0:T(8,128)} %inner_rows.1), calls=%async_computation | async-start | bytes 524288 | tf_op jit(solution)/shard_map/all_to_all | solution.py:554
  27.7 0.0 copy-done.1
  27.7 0.0 copy-done.4
  27.7 0.0 copy-done.5
  27.7 0.0 copy-done
  27.7 0.0 copy-start.3
  27.7 0.9 %outer_zonal.1 = (f32[48,1152]{1,0:T(8,128)S(1)}, f32[16,1152]{1,0:T(8,128)S(1)}) custom-call(f32[864,128]{1,0:T(8,128)S(1)} %bitcast.7, f32[108,1,128]{2,1,0:T(1,128)S(1)} %bitcast.11, f32[108,1,128]{2,1,0:T(1,128)S(1)} %bitcast.17, bf16[2,4,256,256]{3,2,1,0:T(8,128)(2,1)S(1)} %copy-done.1, bf16[2,128,128]{2,1,0:T(8,128)(2,1)S(1)} %copy-done.4, ...), custom_call_target="tpu_custom_call" | custom-call | flops 20000000000 | bytes 10000000000 | tf_op jit(solution)/shard_map/outer_zonal/pallas_call | solution.py:555
  28.6 0.7 %collective-permute-done.odd_ref = f32[256,128]{1,0:T(8,128)S(1)} collective-permute-done((f32[256,128]{1,0:T(8,128)}, f32[256,128]{1,0:T(8,128)S(1)}, u32[]{:S(2)}, u32[]{:S(2)}) %collective-permute-start) | collective-permute-done | bytes 131104 | tf_op jit(solution)/shard_map/ppermute | solution.py:534
  29.3 7.1 %collective-permute-done.1.even_ref = f32[256,128]{1,0:T(8,128)S(1)} collective-permute-done((f32[256,128]{1,0:T(8,128)}, f32[256,128]{1,0:T(8,128)S(1)}, u32[]{:S(2)}, u32[]{:S(2)}) %collective-permute-start.1) | collective-permute-done | bytes 131104 | tf_op jit(solution)/shard_map/ppermute | solution.py:535
  36.5 0.9 %outer_rows.1 = f32[8,64,128]{2,1,0:T(8,128)S(1)} custom-call(f32[864,128]{1,0:T(8,128)S(1)} %bitcast.8, f32[48,1152]{1,0:T(8,128)S(1)} %get-tuple-element.10.z_ref, f32[16,1152]{1,0:T(8,128)S(1)} %get-tuple-element.11.base_ref, f32[108,1,128]{2,1,0:T(1,128)S(1)} %bitcast.12, f32[108,1,128]{2,1,0:T(1,128)S(1)} %bitcast.15, ...), custom_call_target="tpu_custom_call" | custom-call | tf_op jit(solution)/shard_map/outer_rows/pallas_call | solution.py:567
  37.4 0.0 copy-start.7
  37.4 2.5 %all-to-all-done.first_ref = f32[8,64,128]{2,1,0:T(8,128)S(1)} async-done(((f32[8,64,128]{2,1,0:T(8,128)}), f32[8,64,128]{2,1,0:T(8,128)S(1)}, u32[]{:S(2)}, u32[]{:S(2)}) %all-to-all-start) | async-done | bytes 262176 | tf_op jit(solution)/shard_map/all_to_all | solution.py:554
  39.9 12.3 %all_to_all.10.second_ref = f32[8,64,128]{2,1,0:T(8,128)S(1)} all-to-all(f32[8,64,128]{2,1,0:T(8,128)S(1)} %outer_rows.1), channel_id=1, replica_groups=mesh['lat'=64,'lev'=8] {'lev'}, dimensions={0} | all-to-all | bytes 524288 | tf_op jit(solution)/shard_map/all_to_all | solution.py:579
  52.2 2.1 %remap.1 = (f32[8,12,8,144]{3,2,1,0:T(8,128)}, f32[12,144]{1,0:T(8,128)}) custom-call(f32[8]{0:T(128)S(1)} %copy-done.7, f32[8,64,128]{2,1,0:T(8,128)S(1)} %all-to-all-done.first_ref, f32[8,64,128]{2,1,0:T(8,128)S(1)} %all_to_all.10.second_ref), custom_call_target="tpu_custom_call" | custom-call | tf_op jit(solution)/shard_map/remap/pallas_call | solution.py:580
  (4 shorter events, 0.0 us)
Async XLA Ops:
  2.4 26.9 %collective-permute-start = (f32[256,128]{1,0:T(8,128)}, f32[256,128]{1,0:T(8,128)S(1)}, u32[]{:S(2)}, u32[]{:S(2)}) collective-permute-start(f32[256,128]{1,0:T(8,128)} %get-tuple-element.8._odd), channel_id=1, source_target_pairs={{8,16},{24,32},{40,48},{56,64},{72,80},{88,96},{104,112},{120,128}... | collective-permute-start | bytes 393224 | tf_op jit(solution)/shard_map/ppermute | solution.py:534
  17.9 18.6 %collective-permute-start.1 = (f32[256,128]{1,0:T(8,128)}, f32[256,128]{1,0:T(8,128)S(1)}, u32[]{:S(2)}, u32[]{:S(2)}) collective-permute-start(f32[256,128]{1,0:T(8,128)} %get-tuple-element.9._even), channel_id=1, source_target_pairs={{0,8},{16,24},{32,40},{48,56},{64,72},{80,88},{96,104},{112,120},{... | collective-permute-start | bytes 393224 | tf_op jit(solution)/shard_map/ppermute | solution.py:535
  20.6 7.0 %copy-start.1 = (bf16[2,4,256,256]{3,2,1,0:T(8,128)(2,1)S(1)}, bf16[2,4,256,256]{3,2,1,0:T(8,128)(2,1)}, u32[]{:S(2)}) copy-start(bf16[2,4,256,256]{3,2,1,0:T(8,128)(2,1)} %constant.6.clone.wide_far.wide_ref) | copy-start | bytes 3145732
  20.6 7.0 %copy-start.4 = (bf16[2,128,128]{2,1,0:T(8,128)(2,1)S(1)}, bf16[2,128,128]{2,1,0:T(8,128)(2,1)}, u32[]{:S(2)}) copy-start(bf16[2,128,128]{2,1,0:T(8,128)(2,1)} %constant.7.clone.zero_far.zero_ref) | copy-start | bytes 196612
  20.6 7.0 %copy-start.5 = (f32[1,12,1152]{2,0,1:T(1,128)S(1)}, f32[1,12,1152]{2,0,1:T(1,128)}, u32[]{:S(2)}) copy-start(f32[1,12,1152]{2,0,1:T(1,128)} %param.10) | copy-start | bytes 165892
  24.1 3.6 %copy-start = (f32[8,1,12,1152]{3,1,2,0:T(1,128)S(1)}, f32[8,1,12,1152]{3,1,2,0:T(1,128)}, u32[]{:S(2)}) copy-start(f32[8,1,12,1152]{3,1,2,0:T(1,128)} %param.8) | copy-start | bytes 1327108
  24.1 3.6 %copy-start.2 = (f32[1,12,1152]{2,0,1:T(1,128)S(1)}, f32[1,12,1152]{2,0,1:T(1,128)}, u32[]{:S(2)}) copy-start(f32[1,12,1152]{2,0,1:T(1,128)} %param.9) | copy-start | bytes 165892
  24.1 3.6 %copy-start.6 = (f32[8,640]{1,0:T(8,128)S(1)}, f32[8,640]{1,0:T(8,128)}, u32[]{:S(2)}) copy-start(f32[8,640]{1,0:T(8,128)} %constant.8.clone.table_far.table_ref) | copy-start | bytes 61444
  24.1 15.8 %all-to-all-start = ((f32[8,64,128]{2,1,0:T(8,128)}), f32[8,64,128]{2,1,0:T(8,128)S(1)}, u32[]{:S(2)}, u32[]{:S(2)}) async-start(f32[8,64,128]{2,1,0:T(8,128)} %inner_rows.1), calls=%async_computation | async-start | bytes 524288 | tf_op jit(solution)/shard_map/all_to_all | solution.py:554
  27.7 8.7 %copy-start.3 = (f32[1,12,1152]{2,0,1:T(1,128)S(1)}, f32[1,12,1152]{2,0,1:T(1,128)}, u32[]{:S(2)}) copy-start(f32[1,12,1152]{2,0,1:T(1,128)} %param.11) | copy-start | bytes 165892
  37.4 14.8 %copy-start.7 = (f32[8]{0:T(128)S(1)}, f32[8]{0:T(128)}, u32[]{:S(2)}) copy-start(f32[8]{0:T(128)} %weight_ref.1) | copy-start | bytes 100

commit v5 on v3

--- a/solution.py
+++ b/solution.py
@@ -27,7 +27,6 @@
 ZFLOPS = 2 * 10**10
 ZBYTES = 10**10
 WHOLE = 62
-RFLOPS = 10000000000
 F32 = jnp.float32
 BF16 = jnp.bfloat16
 
@@ -469,56 +468,46 @@
     pack_message(OUTER, ratio_row, new_thick, msg)
 
 
-def remap_half(rows, places, weight_ref, in_ref, out_ref, mass_ref, inter_scr):
+def remap_kernel(weight_ref, first_ref, second_ref, out_ref, mass_ref, inter_scr):
     weight_sum = weight_ref[0]
     for k in range(1, NLEV):
         weight_sum = weight_sum + weight_ref[k]
     base = 8 * HALF + 8
-    thick = [in_ref[i, base : base + 8, :] for i in range(NLEV)]
-    upper, lower = [thick[0]], []
-    for i in range(1, NLEV):
-        upper.append(upper[-1] + thick[i])
-    for i in range(NLEV):
-        lower.append(upper[i] - thick[i])
-    total = upper[-1]
-    for v, r in enumerate(rows):
-        mass_ref[r : r + 1, 0:LANES] = total[v : v + 1]
-        mass_ref[r : r + 1, LANES:PIECE] = turn(total[HALF : HALF + 1], -TAIL * v)[:, :TAIL]
-    reach = None
-    for k in range(NLEV):
-        target = total * (weight_ref[k] / weight_sum)
-        reach = target if reach is None else reach + target
-        start = reach - target
-        scale = 1.0 / target
+    for in_ref, rows in ((first_ref, INNER), (second_ref, OUTER)):
+        thick = [in_ref[i, base : base + 8, :] for i in range(NLEV)]
+        upper, lower = [thick[0]], []
+        for i in range(1, NLEV):
+            upper.append(upper[-1] + thick[i])
         for i in range(NLEV):
-            overlap = jnp.minimum(upper[i], reach) - jnp.maximum(lower[i], start)
-            at = 8 * (NLEV * i + k)
-            inter_scr[at : at + 8, :] = jnp.maximum(overlap, 0.0) * scale
-    for v in range(HALF + 1):
-        moved = [None] * NT
-        for i in range(NLEV):
-            share = inter_scr[pl.ds(8 * NLEV * i + v, NLEV, stride=8), :]
+            lower.append(upper[i] - thick[i])
+        total = upper[-1]
+        for v, r in enumerate(rows):
+            mass_ref[r : r + 1, 0:LANES] = total[v : v + 1]
+            mass_ref[r : r + 1, LANES:PIECE] = turn(total[HALF : HALF + 1], -TAIL * v)[:, :TAIL]
+        reach = None
+        for k in range(NLEV):
+            target = total * (weight_ref[k] / weight_sum)
+            reach = target if reach is None else reach + target
+            start = reach - target
+            scale = 1.0 / target
+            for i in range(NLEV):
+                overlap = jnp.minimum(upper[i], reach) - jnp.maximum(lower[i], start)
+                at = 8 * (NLEV * i + k)
+                inter_scr[at : at + 8, :] = jnp.maximum(overlap, 0.0) * scale
+        for v in range(HALF + 1):
+            moved = [None] * NT
+            for i in range(NLEV):
+                share = inter_scr[pl.ds(8 * NLEV * i + v, NLEV, stride=8), :]
+                for t in range(NT):
+                    at = 8 * v + t
+                    term = jnp.broadcast_to(in_ref[i, at : at + 1, :], (NLEV, LANES)) * share
+                    moved[t] = term if i == 0 else moved[t] + term
             for t in range(NT):
-                at = 8 * v + t
-                term = jnp.broadcast_to(in_ref[i, at : at + 1, :], (NLEV, LANES)) * share
-                moved[t] = term if i == 0 else moved[t] + term
-        for t in range(NT):
-            if v < HALF:
-                out_ref[t, places[v], :, 0:LANES] = moved[t]
-            else:
-                for u in range(HALF):
-                    out_ref[t, places[u], :, LANES:PIECE] = turn(moved[t], -TAIL * u)[:, :TAIL]
-
-
-def inner_remap_kernel(weight_ref, in_ref, out_ref, mass_ref, inter_scr):
-    mass_ref[...] = jnp.zeros(mass_ref.shape, F32)
-    remap_half(INNER, range(HALF), weight_ref, in_ref, out_ref, mass_ref, inter_scr)
-
-
-def outer_remap_kernel(weight_ref, in_ref, inner_ref, inner_mass, out_ref, mass_ref, inter_scr):
-    mass_ref[...] = inner_mass[...]
-    out_ref[:, HALO : ROWS - HALO] = inner_ref[...]
-    remap_half(OUTER, OUTER, weight_ref, in_ref, out_ref, mass_ref, inter_scr)
+                if v < HALF:
+                    out_ref[t, rows[v], :, 0:LANES] = moved[t]
+                else:
+                    for u, r in enumerate(rows):
+                        out_ref[t, r, :, LANES:PIECE] = turn(moved[t], -TAIL * u)[:, :TAIL]
 
 
 def swaps(first, bands):
@@ -604,26 +593,15 @@
         name="outer_rows",
     )(q_in, z, base, h_in, cy_in, odd, even)
     second = lax.all_to_all(second, "lev", split_axis=0, concat_axis=0, tiled=True)
-    smem = pl.BlockSpec(memory_space=pltpu.SMEM)
-    inner_out, inner_mass = pl.pallas_call(
-        inner_remap_kernel,
-        out_shape=(shape(NT, HALF, NLEV, PIECE), shape(ROWS, PIECE)),
-        in_specs=[smem, vmem()],
+    remapped, column_mass = pl.pallas_call(
+        remap_kernel,
+        out_shape=(shape(NT, ROWS, NLEV, PIECE), shape(ROWS, PIECE)),
+        in_specs=[pl.BlockSpec(memory_space=pltpu.SMEM), vmem(), vmem()],
         out_specs=(vmem(),) * 2,
         scratch_shapes=[scratch(NLEV * NLEV * 8, LANES)],
         compiler_params=params(32),
-        cost_estimate=pl.CostEstimate(flops=RFLOPS, bytes_accessed=RFLOPS, transcendentals=0),
-        name="inner_remap",
-    )(level_weights, first)
-    remapped, column_mass = pl.pallas_call(
-        outer_remap_kernel,
-        out_shape=(shape(NT, ROWS, NLEV, PIECE), shape(ROWS, PIECE)),
-        in_specs=[smem] + [vmem()] * 3,
-        out_specs=(vmem(),) * 2,
-        scratch_shapes=[scratch(NLEV * NLEV * 8, LANES)],
-        compiler_params=params(32),
-        name="outer_remap",
-    )(level_weights, second, inner_out, inner_mass)
+        name="remap",
+    )(level_weights, first, second)
     return jnp.transpose(remapped, (0, 2, 1, 3)), column_mass
 
 

time: 54.7 us -> 54.8 us (level)
  blocking collectives: 0 us -> 14.1 us
  waiting for transfers between devices: 19.9 us -> 11.5 us
  starting transfers between devices: 23.1 us -> 18.7 us
  Pallas kernels: 10 us -> 8.86 us
    all_to_all x0 -> x1, blocking collectives: none -> 14.1 us  [local(): lax.all_to_all(second, 'lev', split_axis=0, concat_axis=0, tiled=True)]
    all_to_all x1 -> x0, waiting for transfers between devices: 8.87 us -> none  [local(): lax.all_to_all(second, 'lev', split_axis=0, concat_axis=0, tiled=True)]
    all_to_all x1 -> x0, starting transfers between devices: 4.42 us -> none  [local(): lax.all_to_all(second, 'lev', split_axis=0, concat_axis=0, tiled=True)]
    pallas_call x1, Pallas kernels: 1.58 us -> 0.87 us  [local(): pl.pallas_call(outer_kernel, out_shape=shape(NLEV, MSG, LANES), in_specs=...]
    pallas_call x2 -> x1, Pallas kernels: 2.61 us -> 2.13 us  [local(): pl.pallas_call(remap_kernel, out_shape=(shape(NT, ROWS, NLEV, PIECE), sha...]
  transfers between devices with their start and end apart: 4 -> 3, of which waited for: 3 -> 3; matrix products, arithmetic and copies ran while one was open for 0% -> 0% of each run, Pallas kernels for 6% -> 3%
where the time goes in v5:
time: 54.8 us; the launch traced here: 54 us
  starting transfers between devices  18.7 us (34%)
  blocking collectives  14.1 us (26%)
  waiting for transfers between devices  11.5 us (21%)
  Pallas kernels  8.86 us (16%)
  between operations  0.8 us (1%)
    all_to_all x1, blocking collectives, local(): lax.all_to_all(second, 'lev', split_axis=0, concat_axis=0, tiled=True)  14.1 us
    ppermute x1, starting transfers between devices, local(): odd = lax.ppermute(odd, 'lat', swaps(1, bands))  12.4 us
    ppermute x1, waiting for transfers between devices, local(): even = lax.ppermute(even, 'lat', swaps(0, bands))  7.4 us
    pallas_call x1, Pallas kernels, local(): pl.pallas_call(edge_kernel, out_shape=(shape(SEND, LANES),) * 2 + (shape(...  4.87 us
    ppermute x1, waiting for transfers between devices, local(): odd = lax.ppermute(odd, 'lat', swaps(1, bands))  3.67 us
    all_to_all x1, starting transfers between devices, local(): lax.all_to_all(first, 'lev', split_axis=0, concat_axis=0, tiled=True)  3.56 us
    ppermute x1, starting transfers between devices, local(): even = lax.ppermute(even, 'lat', swaps(0, bands))  2.75 us
    pallas_call x1, Pallas kernels, local(): pl.pallas_call(remap_kernel, out_shape=(shape(NT, ROWS, NLEV, PIECE), sha...  2.13 us
  transfers between devices with their start and end apart: 3, of which 3 were waited for; matrix products, arithmetic and copies ran while one was open for 0% of the time, Pallas kernels for 3%

profile of v5, /device:TPU:6, one launch (start us, length us, event | category | flops | bytes accessed | tf_op | source)
XLA Modules:
  0.0 54.0 jit_solution(4817331602264640790)
XLA Ops:
  0.6 4.9 %edge_rows.1 = (f32[256,128]{1,0:T(8,128)}, f32[256,128]{1,0:T(8,128)}, f32[8,64,128]{2,1,0:T(8,128)}) custom-call(f32[864,128]{1,0:T(8,128)} %bitcast.5, f32[108,1,128]{2,1,0:T(1,128)} %bitcast.9, f32[108,1,128]{2,1,0:T(1,128)} %bitcast.13, f32[108,1,128]{2,1,0:T(1,128)} %bitcast.16, bf16[2,4,256,256]{3,2,1,0:T(8,128)(2,1)} %constant.6.clone.refs_4_.wide_ref, ...), custom_call_target="tpu_custom_call" | custom-call | tf_op jit(solution)/shard_map/edge_rows/pallas_call | solution.py:547
  5.5 12.4 %collective-permute-start = (f32[256,128]{1,0:T(8,128)}, f32[256,128]{1,0:T(8,128)S(1)}, u32[]{:S(2)}, u32[]{:S(2)}) collective-permute-start(f32[256,128]{1,0:T(8,128)} %get-tuple-element.10.refs_8_), channel_id=1, source_target_pairs={{8,16},{24,32},{40,48},{56,64},{72,80},{88,96},{104,112},{120,128}... | collective-permute-start | bytes 393224 | tf_op jit(solution)/shard_map/ppermute | solution.py:557
  17.9 2.7 %collective-permute-start.1 = (f32[256,128]{1,0:T(8,128)}, f32[256,128]{1,0:T(8,128)S(1)}, u32[]{:S(2)}, u32[]{:S(2)}) collective-permute-start(f32[256,128]{1,0:T(8,128)} %get-tuple-element.11.refs_9_), channel_id=1, source_target_pairs={{0,8},{16,24},{32,40},{48,56},{64,72},{80,88},{96,104},{112,120},{... | collective-permute-start | bytes 393224 | tf_op jit(solution)/shard_map/ppermute | solution.py:558
  20.7 0.0 copy-start
  20.7 0.0 copy-start.4
  20.7 0.0 copy-start.5
  20.7 0.1 inner_rows.1
  20.8 0.0 copy-start.1
  20.8 0.0 copy-start.2
  20.8 0.0 copy-start.6
  20.9 3.6 %all-to-all-start = ((f32[8,64,128]{2,1,0:T(8,128)}), f32[8,64,128]{2,1,0:T(8,128)S(1)}, u32[]{:S(2)}, u32[]{:S(2)}) async-start(f32[8,64,128]{2,1,0:T(8,128)} %inner_rows.1), calls=%async_computation | async-start | bytes 524288 | tf_op jit(solution)/shard_map/all_to_all | solution.py:570
  24.4 0.0 copy-done
  24.4 0.0 copy-done.4
  24.4 0.0 copy-done.5
  24.4 0.0 copy-done.1
  24.5 0.0 copy-start.3
  24.5 0.9 %outer_zonal.1 = (f32[48,1152]{1,0:T(8,128)S(1)}, f32[16,1152]{1,0:T(8,128)S(1)}) custom-call(f32[864,128]{1,0:T(8,128)S(1)} %bitcast.7, f32[108,1,128]{2,1,0:T(1,128)S(1)} %bitcast.11, f32[108,1,128]{2,1,0:T(1,128)S(1)} %bitcast.18, bf16[2,4,256,256]{3,2,1,0:T(8,128)(2,1)S(1)} %copy-done, bf16[2,128,128]{2,1,0:T(8,128)(2,1)S(1)} %copy-done.4, ...), custom_call_target="tpu_custom_call" | custom-call | flops 20000000000 | bytes 10000000000 | tf_op jit(solution)/shard_map/outer_zonal/pallas_call | solution.py:571
  25.4 3.7 %collective-permute-done.odd_ref = f32[256,128]{1,0:T(8,128)S(1)} collective-permute-done((f32[256,128]{1,0:T(8,128)}, f32[256,128]{1,0:T(8,128)S(1)}, u32[]{:S(2)}, u32[]{:S(2)}) %collective-permute-start) | collective-permute-done | bytes 131104 | tf_op jit(solution)/shard_map/ppermute | solution.py:557
  29.1 7.4 %collective-permute-done.1.even_ref = f32[256,128]{1,0:T(8,128)S(1)} collective-permute-done((f32[256,128]{1,0:T(8,128)}, f32[256,128]{1,0:T(8,128)S(1)}, u32[]{:S(2)}, u32[]{:S(2)}) %collective-permute-start.1) | collective-permute-done | bytes 131104 | tf_op jit(solution)/shard_map/ppermute | solution.py:558
  36.5 0.9 %outer_rows.1 = f32[8,64,128]{2,1,0:T(8,128)S(1)} custom-call(f32[864,128]{1,0:T(8,128)S(1)} %bitcast.8, f32[48,1152]{1,0:T(8,128)S(1)} %get-tuple-element.12.z_ref, f32[16,1152]{1,0:T(8,128)S(1)} %get-tuple-element.13.base_ref, f32[108,1,128]{2,1,0:T(1,128)S(1)} %bitcast.12, f32[108,1,128]{2,1,0:T(1,128)S(1)} %bitcast.15, ...), custom_call_target="tpu_custom_call" | custom-call | tf_op jit(solution)/shard_map/outer_rows/pallas_call | solution.py:583
  37.3 0.0 copy-start.7
  37.4 0.4 all-to-all-done.first_ref
  37.8 14.1 %all_to_all.10.second_ref = f32[8,64,128]{2,1,0:T(8,128)S(1)} all-to-all(f32[8,64,128]{2,1,0:T(8,128)S(1)} %outer_rows.1), channel_id=1, replica_groups=mesh['lat'=64,'lev'=8] {'lev'}, dimensions={0} | all-to-all | bytes 524288 | tf_op jit(solution)/shard_map/all_to_all | solution.py:595
  51.9 2.1 %remap.1 = (f32[8,12,8,144]{3,2,1,0:T(8,128)}, f32[12,144]{1,0:T(8,128)}) custom-call(f32[8]{0:T(128)S(1)} %copy-done.7, f32[8,64,128]{2,1,0:T(8,128)S(1)} %all-to-all-done.first_ref, f32[8,64,128]{2,1,0:T(8,128)S(1)} %all_to_all.10.second_ref), custom_call_target="tpu_custom_call" | custom-call | tf_op jit(solution)/shard_map/remap/pallas_call | solution.py:596
  (4 shorter events, 0.0 us)
Async XLA Ops:
  5.5 23.5 %collective-permute-start = (f32[256,128]{1,0:T(8,128)}, f32[256,128]{1,0:T(8,128)S(1)}, u32[]{:S(2)}, u32[]{:S(2)}) collective-permute-start(f32[256,128]{1,0:T(8,128)} %get-tuple-element.10.refs_8_), channel_id=1, source_target_pairs={{8,16},{24,32},{40,48},{56,64},{72,80},{88,96},{104,112},{120,128}... | collective-permute-start | bytes 393224 | tf_op jit(solution)/shard_map/ppermute | solution.py:557
  17.9 18.5 %collective-permute-start.1 = (f32[256,128]{1,0:T(8,128)}, f32[256,128]{1,0:T(8,128)S(1)}, u32[]{:S(2)}, u32[]{:S(2)}) collective-permute-start(f32[256,128]{1,0:T(8,128)} %get-tuple-element.11.refs_9_), channel_id=1, source_target_pairs={{0,8},{16,24},{32,40},{48,56},{64,72},{80,88},{96,104},{112,120},{... | collective-permute-start | bytes 393224 | tf_op jit(solution)/shard_map/ppermute | solution.py:558
  20.7 3.7 %copy-start = (bf16[2,4,256,256]{3,2,1,0:T(8,128)(2,1)S(1)}, bf16[2,4,256,256]{3,2,1,0:T(8,128)(2,1)}, u32[]{:S(2)}) copy-start(bf16[2,4,256,256]{3,2,1,0:T(8,128)(2,1)} %constant.6.clone.refs_4_.wide_ref) | copy-start | bytes 3145732
  20.7 3.7 %copy-start.4 = (bf16[2,128,128]{2,1,0:T(8,128)(2,1)S(1)}, bf16[2,128,128]{2,1,0:T(8,128)(2,1)}, u32[]{:S(2)}) copy-start(bf16[2,128,128]{2,1,0:T(8,128)(2,1)} %constant.7.clone.refs_5_.zero_ref) | copy-start | bytes 196612
  20.7 3.7 %copy-start.5 = (f32[1,12,1152]{2,0,1:T(1,128)S(1)}, f32[1,12,1152]{2,0,1:T(1,128)}, u32[]{:S(2)}) copy-start(f32[1,12,1152]{2,0,1:T(1,128)} %param.10) | copy-start | bytes 165892
  20.8 3.6 %copy-start.1 = (f32[8,1,12,1152]{3,1,2,0:T(1,128)S(1)}, f32[8,1,12,1152]{3,1,2,0:T(1,128)}, u32[]{:S(2)}) copy-start(f32[8,1,12,1152]{3,1,2,0:T(1,128)} %param.8) | copy-start | bytes 1327108
  20.8 3.6 %copy-start.2 = (f32[1,12,1152]{2,0,1:T(1,128)S(1)}, f32[1,12,1152]{2,0,1:T(1,128)}, u32[]{:S(2)}) copy-start(f32[1,12,1152]{2,0,1:T(1,128)} %param.9) | copy-start | bytes 165892
  20.8 3.6 %copy-start.6 = (f32[8,640]{1,0:T(8,128)S(1)}, f32[8,640]{1,0:T(8,128)}, u32[]{:S(2)}) copy-start(f32[8,640]{1,0:T(8,128)} %constant.8.clone.refs_6_.table_ref) | copy-start | bytes 61444
  20.9 16.9 %all-to-all-start = ((f32[8,64,128]{2,1,0:T(8,128)}), f32[8,64,128]{2,1,0:T(8,128)S(1)}, u32[]{:S(2)}, u32[]{:S(2)}) async-start(f32[8,64,128]{2,1,0:T(8,128)} %inner_rows.1), calls=%async_computation | async-start | bytes 524288 | tf_op jit(solution)/shard_map/all_to_all | solution.py:570
  24.5 12.0 %copy-start.3 = (f32[1,12,1152]{2,0,1:T(1,128)S(1)}, f32[1,12,1152]{2,0,1:T(1,128)}, u32[]{:S(2)}) copy-start(f32[1,12,1152]{2,0,1:T(1,128)} %param.11) | copy-start | bytes 165892
  37.3 14.5 %copy-start.7 = (f32[8]{0:T(128)S(1)}, f32[8]{0:T(128)}, u32[]{:S(2)}) copy-start(f32[8]{0:T(128)} %weight_ref.1) | copy-start | bytes 100
